TPU v7x, 128 devices: a whole 4x4x4 slice. The times are simulated.
128 devices in a mesh: dp: 32 (over x, y, core), seq: 4 (over z).
Axes of the slice: x: 4, y: 4, z: 4, core: 2. Of those that a mesh axis runs over, the one named last changes fastest.
Arguments:
- tokens: bfloat16 [32, 512, 1280], P('dp', 'seq'), may hold values from -6 to 6
- segment_ids: int32 [32, 512], P('dp', 'seq'), may hold values from 0 to 7, never falling along the last dimension, each value on 1 to 384 neighbouring positions
- expert_ids: int32 [32, 512, 2], P('dp', 'seq'), may hold values from 0 to 31, all different within a row; in each aligned block of 128 rows (0 to 127, 128 to 255, ..., all dimensions but the last counted through in order) at most 9 rows name the same one
- gate_values: float32 [32, 512, 2], P('dp', 'seq'), may hold values from 0.2 to 1
- ln_attn: float32 [1280], replicated, may hold values from 0.4 to 1.6
- w_qkv: bfloat16 [1280, 3840], replicated, may hold values from -1 to 1
- w_attn_out: bfloat16 [1280, 1280], replicated, may hold values from -0.15625 to 0.15625
- ln_expert: float32 [1280], replicated, may hold values from 0.4 to 1.6
- w_in: bfloat16 [32, 1280, 5120], P('dp', None, 'seq'), may hold values from -0.15625 to 0.15625
- w_out: bfloat16 [32, 5120, 1280], P('dp', 'seq'), may hold values from -0.078125 to 0.078125
Outputs:
- encoded: bfloat16 [32, 512, 1280], P('dp', 'seq')
Inputs may be any that keep to these rules, and one draw needn't show every extreme that they name: `segment_ids`: segment numbers never fall along a pack; each image holds 1 to 384 patches and one image of each pack exactly 384. `expert_ids`: a patch's two experts differ; among the patches of one device no expert is named more than 9 times, a bound that some block reaches.
All inputs are finite; a program needn't handle non-finite values.
Results may differ from a plain program's by a relative error of at most 0.009.
Values may be sent and summed in bfloat16 or wider, within the bound.
A program may use at most 128 MiB of HBM per device.

v0:
```python
import jax
import jax.numpy as jnp
from jax import lax
from jax.sharding import PartitionSpec as P

HEADS = 16
HEAD_DIM = 80
TOP = 2


epsilon = 1e-06


def normalize(rows, gain):
    mean = jnp.mean(rows, axis=-1, keepdims=True)
    centered = rows - mean
    spread = jnp.mean(centered * centered, axis=-1, keepdims=True)
    return centered * lax.rsqrt(spread + epsilon) * gain


def expert_rows(slot_rows, first, second):
    hidden = jax.nn.gelu(jnp.dot(slot_rows, first, preferred_element_type=jnp.float32)).astype(
        jnp.bfloat16
    )
    return jnp.dot(hidden, second, preferred_element_type=jnp.float32)


def body(
    tokens, segment_ids, expert_ids, gate_values, ln_attn, w_qkv, w_attn_out, ln_expert, w_in, w_out
):
    width = tokens.shape[2]
    count = tokens.shape[1]
    scale = HEAD_DIM ** (-0.5)
    patches = tokens[0].astype(jnp.float32)
    attn_in = normalize(patches, ln_attn).astype(jnp.bfloat16)
    qkv = jnp.dot(attn_in, w_qkv, preferred_element_type=jnp.float32).astype(jnp.bfloat16)
    queries = qkv[:, :width].reshape(count, HEADS, HEAD_DIM)
    own_keys = qkv[:, width : 2 * width]
    own_values = qkv[:, 2 * width :]
    query_seg = segment_ids[0].astype(jnp.bfloat16)
    run_max = jnp.full((HEADS, count), -1e30, jnp.float32)
    keys = lax.all_gather(own_keys, "seq", axis=0, tiled=True)
    values = lax.all_gather(own_values, "seq", axis=0, tiled=True)
    key_seg = lax.all_gather(query_seg, "seq", axis=0, tiled=True)
    length = keys.shape[0]
    keys = keys.reshape(length, HEADS, HEAD_DIM)
    values = values.reshape(length, HEADS, HEAD_DIM)
    scores = jnp.einsum("qhd,khd->hqk", queries, keys, preferred_element_type=jnp.float32) * scale
    allowed = (query_seg[:, None] == key_seg[None, :])[None]
    scores = jnp.where(allowed, scores, -1e30)
    new_max = jnp.maximum(run_max, jnp.max(scores, axis=-1))
    weights = jnp.where(allowed, jnp.exp(scores - new_max[..., None]), 0.0)
    run_sum = jnp.sum(weights, axis=-1)
    update = jnp.einsum(
        "hqk,khd->hqd", weights.astype(jnp.bfloat16), values, preferred_element_type=jnp.float32
    )
    accum = update
    run_max, run_sum, accum = (new_max, run_sum, accum)
    context = (
        (accum / run_sum[..., None]).transpose(1, 0, 2).reshape(count, width).astype(jnp.bfloat16)
    )
    middle = patches + jnp.dot(context, w_attn_out, preferred_element_type=jnp.float32)
    expert_in = normalize(middle, ln_expert).astype(jnp.bfloat16)
    experts = lax.axis_size("dp")
    groups = lax.axis_size("seq")
    capacity = max(2, 9 * TOP * count // (8 * experts))
    chosen = expert_ids[0].reshape(count * TOP)
    onehot = (chosen[:, None] == jnp.arange(experts, dtype=jnp.int32)[None, :]).astype(jnp.int32)
    slots = jnp.sum((jnp.cumsum(onehot, axis=0) - onehot) * onehot, axis=1)
    targets = chosen * capacity + slots
    buffer = (
        jnp.zeros((experts * capacity, width), jnp.bfloat16)
        .at[targets]
        .set(jnp.repeat(expert_in, TOP, axis=0))
    )
    buffer = buffer.reshape(experts, capacity, width)
    copies = jnp.broadcast_to(buffer[:, None], (experts, groups, capacity, width)).reshape(
        experts * groups, capacity, width
    )
    arrived = lax.all_to_all(copies, ("dp", "seq"), split_axis=0, concat_axis=0, tiled=True)
    partial_value = expert_rows(arrived.reshape(-1, width), w_in[0], w_out[0]).reshape(
        experts * groups, capacity, width
    )
    coming = lax.all_to_all(
        partial_value.astype(jnp.bfloat16), ("dp", "seq"), split_axis=0, concat_axis=0, tiled=True
    ).astype(partial_value.dtype)
    returned = jnp.sum(coming.reshape(experts, groups, capacity, width), axis=1).astype(
        jnp.bfloat16
    )
    picked = (
        returned.reshape(experts * capacity, width)[targets]
        .astype(jnp.float32)
        .reshape(count, TOP, width)
    )
    mixed = jnp.sum(picked * gate_values[0][..., None], axis=1)
    return (middle + mixed).astype(jnp.bfloat16).reshape(1, count, width)


def solution(mesh):
    placed = (
        P("dp", "seq", None),
        P("dp", "seq"),
        P("dp", "seq", None),
        P("dp", "seq", None),
        P(),
        P(),
        P(),
        P(),
        P("dp", None, "seq"),
        P("dp", "seq", None),
    )
    return jax.shard_map(
        body, mesh=mesh, in_specs=placed, out_specs=P("dp", "seq", None), check_vma=False
    )
```

profile of v0, /device:TPU:1, one launch (start us, length us, event | category | flops | bytes accessed | tf_op | source)
XLA Modules:
  0.0 289.4 jit_solution(15694944273819702499)
XLA Ops:
  6.5 0.0 copy-start
  6.5 0.0 all-gather.4.cloned.1.call-start
  6.5 1.2 convert_reduce_fusion
  7.8 1.2 fusion.32
  9.0 0.0 copy-start.7
  9.0 0.0 copy-start.9
  9.0 5.5 %convolution_convert_fusion = bf16[128,3840]{1,0:T(8,128)(2,1)S(1)} fusion(bf16[1280,3840]{1,0:T(8,128)(2,1)} %param.15, bf16[1,128,1280]{2,1,0:T(8,128)(2,1)} %param.10, f32[1280]{0:T(1024)} %param.14, f32[128]{0:T(128)S(1)} %add_rsqrt_fusion.1, f32[128]{0:T(128)S(1)} %broadcast_multiply_fusion.2), kind=kOutput, calls=%fused_computation.12 | convolution fusion | flops 1259601920 | bytes 11147264 | tf_op jit(solution)/shard_map/dot_general | solution.py:36
  14.5 1.0 fusion.49
  15.5 0.0 all-gather.4.cloned.1.call-update
  15.5 0.0 all-gather.6.cloned.1.call-start
  15.6 0.7 all-gather.6.cloned.1.call-update
  16.3 0.0 copy-done.7
  16.3 0.1 copy.29
  16.4 0.1 eq.49
  16.5 0.1 eq.45
  16.7 1.9 copy.25
  18.6 0.6 reduce-window.6
  19.1 0.2 slice_reduce_fusion
  19.4 0.1 copy.28
  19.5 0.1 mul.103
  19.6 0.0 copy-done.9
  19.7 9.8 %all-gather = bf16[1,512]{1,0:T(2,128)(2,1)S(1)} all-gather(bf16[1,128]{1,0:T(2,128)(2,1)S(1)} %get-tuple-element.9), channel_id=2, replica_groups=mesh['dp'=32,'seq'=4] {'seq'}, dimensions={1}, use_global_device_ids=true | all-gather | bytes 1280 | tf_op jit(solution)/shard_map/all_gather | solution.py:44
  29.4 0.1 fusion.44
  29.5 0.1 broadcast_compare_fusion
  29.7 13.2 %all-gather.4.cloned.1.call-done = bf16[512,1280]{1,0:T(8,128)(2,1)} async-done(((bf16[128,1280]{1,0:T(8,128)(2,1)}), bf16[512,1280]{1,0:T(8,128)(2,1)}) %all-gather.4.cloned.1.call-update) | async-done | bytes 1310736 | tf_op jit(solution)/shard_map/all_gather | solution.py:42
  42.8 2.4 copy.26
  45.3 2.4 fusion.8
  47.7 0.0 copy-start.2
  47.7 1.9 copy-done.2
  49.6 1.3 fusion.14
  50.9 19.2 %all-gather.6.cloned.1.call-done = bf16[512,1280]{1,0:T(8,128)(2,1)} async-done(((bf16[128,1280]{1,0:T(8,128)(2,1)}), bf16[512,1280]{1,0:T(8,128)(2,1)}) %all-gather.6.cloned.1.call-update) | async-done | bytes 1310736 | tf_op jit(solution)/shard_map/all_gather | solution.py:43
  70.1 2.4 copy.27
  72.5 4.0 %fusion.26 = bf16[128,16,80]{0,2,1:T(8,128)(2,1)S(1)} fusion(bf16[512,16,80]{0,2,1:T(8,128)(2,1)} %bitcast.76, f32[16,128,512]{2,1,0:T(8,128)} %copy-done.2, f32[16,128]{1,0:T(8,128)S(1)} %broadcast_maximum_fusion, pred[128,512]{1,0:T(8,128)(4,1)S(1)} %broadcast_compare_fusion, f32[128,16]{0,1:T(8,128)S(1)} %bitcast.78), kind=kOutput, calls=%fused_computation.29 | convolution fusion | flops 173342720 | bytes 5914624 | tf_op jit(solution)/shard_map/hqk,khd->hqd/dot_general | solution.py:54
  76.5 0.0 copy-done.4
  76.5 0.0 copy-done.5
  76.5 0.7 fusion.50
  77.3 0.0 copy-start.3
  77.3 0.2 multiply_reduce_fusion.1
  77.5 0.6 copy-done.3
  78.1 0.0 copy-done.6
  78.1 0.2 multiply_convert_fusion
  78.3 1.2 broadcast_in_dim.53
  79.5 2.7 reshape.173
  82.2 3.2 %scatter_custom_fusion = bf16[288,1280]{1,0:T(8,128)(2,1)} fusion(s32[256]{0:T(256)S(1)} %bitcast.79, bf16[256,1280]{1,0:T(8,128)(2,1)} %reshape.173, bf16[]{:T(256)} %constant.10.clone.1), kind=kCustom, calls=%fused_computation.41 | custom fusion | bytes 737792 | tf_op jit(solution)/shard_map/scatter | solution.py:74
  85.3 2.3 broadcast_in_dim.54
  87.7 1.7 broadcast_in_dim.55
  89.4 74.3 %all_to_all.10 = bf16[128,9,1280]{2,1,0:T(8,128)(2,1)} all-to-all(bf16[128,9,1280]{2,1,0:T(8,128)(2,1)S(1)} %bitcast.73), channel_id=1, replica_groups=mesh['dp'=32,'seq'=4] {'dp','seq'}, dimensions={0} | all-to-all | bytes 5898240 | tf_op jit(solution)/shard_map/all_to_all | solution.py:80
  163.7 6.0 %reshape.156 = bf16[1152,1280]{1,0:T(8,128)(2,1)} reshape(bf16[128,9,1280]{2,1,0:T(8,128)(2,1)} %all_to_all.10) | data formatting | bytes 5898240 | tf_op jit(solution)/shard_map/reshape | solution.py:81
  169.7 0.0 copy-done
  169.7 8.3 %fusion.7 = bf16[1152,1280]{1,0:T(8,128)(2,1)} fusion(bf16[1152,1280]{1,0:T(8,128)(2,1)} %reshape.156, bf16[1,1280,1280]{2,1,0:T(8,128)(2,1)S(1)} %copy-done), kind=kOutput, calls=%fused_computation.10 | convolution fusion | flops 3788144640 | bytes 9175040 | tf_op jit(solution)/shard_map/dot_general | solution.py:22
  178.1 5.7 %dot_general.28 = bf16[128,9,1280]{2,1,0:T(8,128)(2,1)} reshape(bf16[1152,1280]{1,0:T(8,128)(2,1)} %fusion.7) | data formatting | bytes 5898240 | tf_op jit(solution)/shard_map/dot_general | solution.py:25
  183.8 8.5 %convolution_convert_fusion.1 = bf16[128,9,1280]{2,0,1:T(8,128)(2,1)S(1)} fusion(bf16[1,1280,1280]{2,1,0:T(8,128)(2,1)} %param.19, bf16[128,9,1280]{2,1,0:T(8,128)(2,1)} %dot_general.28), kind=kOutput, calls=%fused_computation.15 | convolution fusion | flops 3776348160 | bytes 9175040 | tf_op jit(solution)/shard_map/dot_general | solution.py:25
  192.4 4.1 %copy.33 = bf16[128,9,1280]{2,1,0:T(8,128)(2,1)} copy(bf16[128,9,1280]{2,0,1:T(8,128)(2,1)S(1)} %convolution_convert_fusion.1) | data formatting | bytes 5898240 | tf_op jit(solution)/shard_map/convert_element_type | solution.py:85
  196.5 5.1 %all-to-all-start.1 = ((bf16[128,9,1280]{2,1,0:T(8,128)(2,1)}), bf16[128,9,1280]{2,1,0:T(8,128)(2,1)}, u32[]{:S(2)}, u32[]{:S(2)}) async-start(bf16[128,9,1280]{2,1,0:T(8,128)(2,1)} %copy.33), calls=%async_computation.1 | async-start | bytes 10485760 | tf_op jit(solution)/shard_map/all_to_all | solution.py:84
  201.6 0.0 copy-done.8
  201.6 0.1 copy.36
  201.7 64.5 %all-to-all-done.1 = bf16[128,9,1280]{2,1,0:T(8,128)(2,1)} async-done(((bf16[128,9,1280]{2,1,0:T(8,128)(2,1)}), bf16[128,9,1280]{2,1,0:T(8,128)(2,1)}, u32[]{:S(2)}, u32[]{:S(2)}) %all-to-all-start.1) | async-done | bytes 2949152 | tf_op jit(solution)/shard_map/all_to_all | solution.py:84
  266.2 3.4 %bitcast_reduce_fusion = bf16[32,9,1280]{2,1,0:T(8,128)(2,1)S(1)} fusion(bf16[128,9,1280]{2,1,0:T(8,128)(2,1)} %all-to-all-done.1), kind=kLoop, calls=%fused_computation.11 | loop fusion | flops 1105920 | bytes 3686400 | tf_op jit(solution)/shard_map/reduce_sum | solution.py:87
  269.7 1.2 convert_element_type.80
  270.9 4.0 %gather_fusion = bf16[256,1280]{1,0:T(8,128)(2,1)} fusion(bf16[288,1280]{1,0:T(8,128)(2,1)} %convert_element_type.80, s32[1024]{0:T(1024)S(1)} %pad_clamp_fusion), kind=kCustom, calls=%fused_computation | custom fusion | bytes 1311744 | tf_op jit(solution)/shard_map/gather | solution.py:91
  274.9 2.8 reshape.160
  277.7 3.0 %multiply_reduce_fusion = f32[128,1280]{1,0:T(8,128)S(1)} fusion(f32[128,2,1280]{2,1,0:T(2,128)} %reshape.160, f32[128,2]{1,0:T(8,128)S(1)} %copy.36), kind=kLoop, calls=%fused_computation.26 | loop fusion | flops 491520 | bytes 1967104 | tf_op jit(solution)/shard_map/reduce_sum | solution.py:95
  280.7 1.9 fusion.37
  282.6 0.0 copy-done.1
  (18 shorter events, 0.1 us)
Async XLA Ops:
  6.5 163.2 %copy-start = (bf16[1,1280,1280]{2,1,0:T(8,128)(2,1)S(1)}, bf16[1,1280,1280]{2,1,0:T(8,128)(2,1)}, u32[]{:S(2)}) copy-start(bf16[1,1280,1280]{2,1,0:T(8,128)(2,1)} %param.18) | copy-start | bytes 9830404
  6.5 36.3 %all-gather.4.cloned.1.call-start = ((), (), s32[]{:S(2)}) async-start(), calls=%async_computation.2 | async-start | bytes 1638400 | tf_op jit(solution)/shard_map/all_gather | solution.py:42
  9.0 7.3 %copy-start.7 = (s32[1,128,2]{1,2,0:T(2,128)S(1)}, s32[1,128,2]{1,2,0:T(2,128)}, u32[]{:S(2)}) copy-start(s32[1,128,2]{1,2,0:T(2,128)} %param.12) | copy-start | bytes 3076
  9.0 10.6 %copy-start.9 = (s32[1,128]{1,0:T(1,128)S(1)}, s32[1,128]{1,0:T(1,128)}, u32[]{:S(2)}) copy-start(s32[1,128]{1,0:T(1,128)} %param.11) | copy-start | bytes 1540
  15.5 54.6 %all-gather.6.cloned.1.call-start = ((), (), s32[]{:S(2)}) async-start(), calls=%async_computation.3 | async-start | bytes 1638400 | tf_op jit(solution)/shard_map/all_gather | solution.py:43
  47.7 1.9 copy-start.2
  72.5 4.0 %copy-start.4 = (bf16[1,128,1280]{2,1,0:T(8,128)(2,1)S(1)}, bf16[1,128,1280]{2,1,0:T(8,128)(2,1)}, u32[]{:S(2)}) copy-start(bf16[1,128,1280]{2,1,0:T(8,128)(2,1)} %param.10) | copy-start | bytes 983044
  72.5 4.0 %copy-start.5 = (bf16[1280,1280]{1,0:T(8,128)(2,1)S(1)}, bf16[1280,1280]{1,0:T(8,128)(2,1)}, u32[]{:S(2)}) copy-start(bf16[1280,1280]{1,0:T(8,128)(2,1)} %param.16) | copy-start | bytes 9830404
  76.5 1.6 copy-start.6
  77.3 0.8 copy-start.3
  196.5 5.1 %copy-start.8 = (f32[1,128,2]{1,2,0:T(2,128)S(1)}, f32[1,128,2]{1,2,0:T(2,128)}, u32[]{:S(2)}) copy-start(f32[1,128,2]{1,2,0:T(2,128)} %param.13) | copy-start | bytes 3076
  196.5 69.7 %all-to-all-start.1 = ((bf16[128,9,1280]{2,1,0:T(8,128)(2,1)}), bf16[128,9,1280]{2,1,0:T(8,128)(2,1)}, u32[]{:S(2)}, u32[]{:S(2)}) async-start(bf16[128,9,1280]{2,1,0:T(8,128)(2,1)} %copy.33), calls=%async_computation.1 | async-start | bytes 10485760 | tf_op jit(solution)/shard_map/all_to_all | solution.py:84
  270.9 11.7 %copy-start.1 = (bf16[1,1280,1280]{2,1,0:T(8,128)(2,1)S(1)}, bf16[1,1280,1280]{2,1,0:T(8,128)(2,1)}, u32[]{:S(2)}) copy-start(bf16[1,1280,1280]{2,1,0:T(8,128)(2,1)} %param.18) | copy-start | bytes 9830404
Sparse Core Ops, SparseCore 0:
  15.6 27.1 all-gather.3
  44.5 25.5 all-gather.5
where the time goes:
time: 290 us; the launch traced here: 289 us
  waiting for transfers between devices  97.6 us (34%)
  blocking collectives  84.1 us (29%)
  local copies, waits for them, and re-layouts  46.3 us (16%)
  matrix products  29.4 us (10%)
  between operations  13.6 us (5%)
  other arithmetic  13.3 us (5%)
  starting transfers between devices  5.13 us (2%)
    all_to_all x1, blocking collectives, body(): lax.all_to_all(copies, ('dp', 'seq'), split_axis=0, concat_axis=0, tiled=...  74.3 us
    all_to_all x1, waiting for transfers between devices, body(): lax.all_to_all(partial_value.astype(jnp.bfloat16), ('dp', 'seq'), split_a...  64.5 us
    all_gather x1, waiting for transfers between devices, body(): values = lax.all_gather(own_values, 'seq', axis=0, tiled=True)  19.2 us
    all_gather x1, waiting for transfers between devices, body(): keys = lax.all_gather(own_keys, 'seq', axis=0, tiled=True)  13.2 us
    all_gather x1, blocking collectives, body(): key_seg = lax.all_gather(query_seg, 'seq', axis=0, tiled=True)  9.76 us
    dot_general x1, matrix products, expert_rows(): return jnp.dot(hidden, second, preferred_element_type=jnp.float32)  8.54 us
    dot_general x1, matrix products, expert_rows(): jnp.dot(slot_rows, first, preferred_element_type=jnp.float32)  8.33 us
    reshape x1, local copies, waits for them, and re-layouts, body(): arrived.reshape(-1, width)  5.99 us
  transfers between devices with their start and end apart: 3, of which 3 were waited for; matrix products, arithmetic and copies ran while one was open for 3% of the time, Pallas kernels for 0%

commit v1 on v0

v1 whole, which is shorter than its diff:
```python
import functools

import jax
import jax.numpy as jnp
from jax import lax
from jax.experimental import pallas as pl
from jax.experimental.pallas import tpu as pltpu
from jax.sharding import PartitionSpec as P

F32 = jnp.float32
BF16 = jnp.bfloat16
I32 = jnp.int32
MESH = pl.DeviceIdType.MESH

D = 1280
HEADS = 16
HEAD = 80
TOK = 128
CAP = 9
NE = 32
COL = 256
NC = D // COL
MSG = 48
HALF = 16
CR = HALF * CAP
ALL = NE * MSG
EPS = 1e-06
NEG = -1e30

GROUPS = (((0, 1, 2), 0), ((3,), 128), ((4, 5), 256), ((6, 7), 384))


def normalize(rows, gain):
    mean = jnp.mean(rows, axis=-1, keepdims=True)
    centered = rows - mean
    spread = jnp.mean(centered * centered, axis=-1, keepdims=True)
    return centered * lax.rsqrt(spread + EPS) * gain


def gelu(x):
    return 0.5 * x * (1.0 + jnp.tanh(0.7978845608028654 * (x + 0.044715 * (x * x * x))))


def iota(shape, dim):
    return lax.broadcasted_iota(I32, shape, dim)


def dot(a, b):
    return jnp.dot(a, b, preferred_element_type=F32)


def cols(j):
    return pl.ds(pl.multiple_of(j * COL, COL), COL)


def kernel(
    tok, seg, eid, gate, lna, lne, wqkv_h, wao_h, win_h, wout_h, out,
    wqkv, wao, win, wout, xn, segs, q, k, v, ctx, ctxb, mid, xp, g, send, rcv, a, hid,
    part, keep, own, stage, back, rst, pack, ret, pick, unp, pkm, gcol,
    w_sem, as_sem, ar_sem, ss_sem, sr_sem, ds_sem, dr_sem, zs_sem, zr_sem, bs_sem, br_sem,
    es_sem, er_sem,
):
    d = lax.axis_index("dp")
    z = lax.axis_index("seq")
    zl = lax.rem(z + 3, 4)
    zr = lax.rem(z + 1, 4)
    zo = lax.rem(z + 2, 4)
    x, y, c = d // 8, lax.rem(d // 2, 4), lax.rem(d, 2)

    def shifted(j, sign):
        dx, dy, dc = j // 8, lax.rem(j // 2, 4), lax.rem(j, 2)
        if sign < 0:
            dx, dy = 4 - dx, 4 - dy
        return lax.rem(x + dx, 4) * 8 + lax.rem(y + dy, 4) * 2 + lax.rem(c + dc, 2)

    def rows48(j):
        return pl.ds(pl.multiple_of(j * MSG, MSG), MSG)

    loads = []
    for i in range(3):
        part_of = pl.ds(i * D, D)
        loads.append(pltpu.make_async_copy(wqkv_h.at[:, part_of], wqkv.at[:, part_of], w_sem.at[i]))
    loads.append(pltpu.make_async_copy(wao_h, wao, w_sem.at[3]))
    loads.append(pltpu.make_async_copy(win_h, win, w_sem.at[4]))
    loads.append(pltpu.make_async_copy(wout_h, wout, w_sem.at[5]))
    for load in loads:
        load.start()

    barrier = pltpu.get_barrier_semaphore()
    for other in (zl, zr, zo):
        pl.semaphore_signal(barrier, inc=1, device_id=(d, other), device_id_type=MESH)

    def greet(j, _):
        pl.semaphore_signal(barrier, inc=1, device_id=(shifted(j, 1), z), device_id_type=MESH)
        return 0

    lax.fori_loop(1, NE, greet, 0)
    xn[pl.ds(0, TOK), :] = normalize(tok[...].astype(F32), lna[...]).astype(BF16)
    segs[0] = jnp.broadcast_to(seg[...], (8, TOK))
    pl.semaphore_wait(barrier, NE - 1 + 3)

    def remote(src, dst, s_sem, r_sem, dev):
        return pltpu.make_async_remote_copy(
            src_ref=src, dst_ref=dst, send_sem=s_sem, recv_sem=r_sem,
            device_id=dev, device_id_type=MESH,
        )

    right, left, across = (d, zr), (d, zl), (d, zo)

    def xrows(slot, half):
        return xn.at[pl.ds(slot * TOK + half * 64, 64), :]

    seg_copies = [
        remote(segs.at[0], segs.at[1], ss_sem.at[0], sr_sem.at[0], right),
        remote(segs.at[0], segs.at[2], ss_sem.at[1], sr_sem.at[1], left),
        remote(segs.at[0], segs.at[3], ss_sem.at[2], sr_sem.at[2], across),
    ]
    r0 = remote(xrows(0, 0), xrows(1, 0), as_sem.at[0], ar_sem.at[0], right)
    r1 = remote(xrows(0, 1), xrows(1, 1), as_sem.at[1], ar_sem.at[1], right)
    l1 = remote(xrows(0, 1), xrows(2, 1), as_sem.at[2], ar_sem.at[2], left)
    l0 = remote(xrows(0, 0), xrows(2, 0), as_sem.at[3], ar_sem.at[3], left)
    ro = remote(xrows(1, 0), xrows(3, 0), as_sem.at[4], ar_sem.at[4], right)
    lo = remote(xrows(2, 1), xrows(3, 1), as_sem.at[5], ar_sem.at[5], left)
    r0.start()
    l1.start()
    r1.start()
    l0.start()
    for copy in seg_copies:
        copy.start()

    e0, e1 = eid[0:1, :], eid[1:2, :]
    ei = iota((NE, TOK), 0)
    named = jnp.where((ei == e0) | (ei == e1), 1.0, 0.0).astype(BF16)
    before = jnp.where(iota((TOK, TOK), 0) < iota((TOK, TOK), 1), 1.0, 0.0).astype(BF16)
    count = dot(named, before)
    s0 = jnp.sum(jnp.where(ei == e0, count, 0.0), axis=0, keepdims=True)
    s1 = jnp.sum(jnp.where(ei == e1, count, 0.0), axis=0, keepdims=True)
    t0 = e0.astype(F32) * MSG + s0
    t1 = e1.astype(F32) * MSG + s1
    ri = iota((TOK, TOK), 0)
    square = jnp.where(
        ri == 0, t0, jnp.where(ri == 1, t1, jnp.where(ri == 2, gate[0:1, :], gate[1:2, :]))
    )
    gcol[...] = jnp.transpose(square)
    t0, t1 = t0.astype(I32), t1.astype(I32)

    def make_g(i, _):
        rows = pl.ds(pl.multiple_of(i * 256, 256), 256)
        r = iota((256, TOK), 0) + i * 256
        for cc in range(NC):
            hit = (r == t0 + CAP * cc) | (r == t1 + CAP * cc)
            g[rows, cc * TOK : (cc + 1) * TOK] = jnp.where(hit, 1.0, 0.0).astype(BF16)
        return 0

    lax.fori_loop(0, ALL // 256, make_g, 0)

    for load in loads[:3]:
        load.wait()

    def own_q(j, _):
        q[:, cols(j)] = dot(xn[pl.ds(0, TOK), :], wqkv[:, cols(j)]).astype(BF16)
        return 0

    lax.fori_loop(0, NC, own_q, 0)

    def keys_values(first, number):
        rows = pl.ds(first, number)

        def step(j, _):
            k[rows, cols(j)] = dot(xn[rows, :], wqkv[:, cols(j + NC)]).astype(BF16)
            v[rows, cols(j)] = dot(xn[rows, :], wqkv[:, cols(j + 2 * NC)]).astype(BF16)
            return 0

        lax.fori_loop(0, NC, step, 0)

    keys_values(0, TOK)
    r0.wait_recv()
    ro.start()
    l1.wait_recv()
    lo.start()

    i = iota((CR, HALF * MSG), 0)
    r = iota((CR, HALF * MSG), 1)
    at = i + (MSG - CAP) * lax.shift_right_logical(i * 57, 9)
    for cc in range(NC):
        unp[pl.ds(cc * CR, CR), :] = jnp.where(r == at + CAP * cc, 1.0, 0.0).astype(BF16)
    i = iota((HALF * MSG, CR), 1)
    r = iota((HALF * MSG, CR), 0)
    at = i + (MSG - CAP) * lax.shift_right_logical(i * 57, 9)
    for cc in range(NC):
        pkm[cc] = jnp.where(r == at + CAP * cc, 1.0, 0.0).astype(BF16)

    r1.wait_recv()
    l0.wait_recv()
    keys_values(TOK, 2 * TOK)

    ri = iota((TOK, ALL), 1)
    c0, c1 = gcol[:, 0:1].astype(I32), gcol[:, 1:2].astype(I32)

    def make_pick(cc, _):
        base = pl.multiple_of(cc * 256, 256)
        pick[pl.ds(base, TOK), :] = jnp.where(ri == c0 + CAP * cc, 1.0, 0.0).astype(BF16)
        pick[pl.ds(base + TOK, TOK), :] = jnp.where(ri == c1 + CAP * cc, 1.0, 0.0).astype(BF16)
        return 0

    lax.fori_loop(0, NC, make_pick, 0)

    for copy in seg_copies:
        copy.wait_recv()
    eight = iota((8, TOK), 0)
    kinds = [jnp.where(eight == segs[s], 1.0, 0.0).astype(BF16) for s in range(4)]
    key_kind = jnp.concatenate(kinds, axis=1)
    same = lax.dot_general(kinds[0], key_kind, (((0,), (0,)), ((), ())), preferred_element_type=F32)
    bias = jnp.where(same > 0.5, 0.0, NEG)

    ro.wait_recv()
    lo.wait_recv()
    keys_values(3 * TOK, TOK)

    scale = HEAD ** (-0.5)
    ctx[...] = jnp.zeros((TOK, D), F32)
    for half in range(2):
        for heads, at in GROUPS:
            window = pl.ds(half * 640 + at, COL)
            lane = iota((TOK, COL), 1) + at
            masks = [(lane >= h * HEAD) & (lane < (h + 1) * HEAD) for h in heads]
            qw = q[:, window]
            zero = jnp.zeros_like(qw)
            stacked = jnp.concatenate([jnp.where(m, qw, zero) for m in masks], axis=0)
            scores = lax.dot_general(
                stacked, k[:, window], (((1,), (1,)), ((), ())), preferred_element_type=F32
            )
            probs, sums = [], []
            for n in range(len(heads)):
                s = scores[n * TOK : (n + 1) * TOK, :] * scale + bias
                w = jnp.exp(s - jnp.max(s, axis=-1, keepdims=True))
                sums.append(jnp.sum(w, axis=-1, keepdims=True))
                probs.append(w.astype(BF16))
            mixed = dot(jnp.concatenate(probs, axis=0), v[:, window])
            total = ctx[:, window]
            for n, m in enumerate(masks):
                total = jnp.where(m, mixed[n * TOK : (n + 1) * TOK, :] / sums[n], total)
            ctx[:, window] = total
    ctxb[...] = ctx[...].astype(BF16)

    loads[3].wait()

    def project(j, _):
        mid[:, cols(j)] = tok[:, cols(j)].astype(F32) + dot(ctxb[...], wao[:, cols(j)])
        return 0

    lax.fori_loop(0, NC, project, 0)
    expert_in = normalize(mid[...], lne[...]).astype(BF16)
    for cc in range(NC):
        xp[pl.ds(cc * TOK, TOK), :] = expert_in[:, cc * COL : (cc + 1) * COL]

    def fill(i, _):
        rows = pl.ds(pl.multiple_of(i * 256, 256), 256)
        send[rows, :] = dot(g[rows, :], xp[...]).astype(BF16)
        return 0

    lax.fori_loop(0, ALL // 256, fill, 0)

    def to_expert(j, _):
        dest = shifted(j, 1)
        remote(
            send.at[rows48(dest), :], rcv.at[rows48(j), :], ds_sem, dr_sem.at[j // HALF], (dest, z)
        ).start()
        return 0

    lax.fori_loop(1, NE, to_expert, 0)
    rcv[pl.ds(0, MSG), :] = send[rows48(d), :]

    loads[4].wait()
    loads[5].wait()

    def chunk(slot, half):
        return a.at[slot, half]

    def unpack(half):
        first, number = (MSG, (HALF - 1) * MSG) if half == 0 else (HALF * MSG, HALF * MSG)
        got = rcv.at[pl.ds(first, number), :]
        remote(got, got, ds_sem, dr_sem.at[half], right).wait_recv()
        for cc in range(NC):
            piece = dot(unp[pl.ds(cc * CR, CR), :], rcv[pl.ds(half * HALF * MSG, HALF * MSG), :])
            a[0, half, :, cc * COL : (cc + 1) * COL] = piece.astype(BF16)

    zc = {}
    for half in range(2):
        zc["r", half] = remote(chunk(0, half), chunk(1, half), zs_sem.at[half], zr_sem.at[half], right)
        zc["l", half] = remote(
            chunk(0, half), chunk(2, half), zs_sem.at[2 + half], zr_sem.at[2 + half], left
        )
    zc["ro"] = remote(chunk(1, 0), chunk(3, 0), zs_sem.at[4], zr_sem.at[4], right)
    zc["lo"] = remote(chunk(2, 1), chunk(3, 1), zs_sem.at[5], zr_sem.at[5], left)

    def expert(slot, half, store):
        def first(j, _):
            hid[:, cols(j)] = gelu(dot(a[slot, half], win[:, cols(j)])).astype(BF16)
            return 0

        lax.fori_loop(0, NC, first, 0)

        def second(j, _):
            store(cols(j), dot(hid[...], wout[:, cols(j)]))
            return 0

        lax.fori_loop(0, NC, second, 0)

    def into_own(half):
        def store(at, value):
            own[half, :, at] = value

        return store

    def into_part(n):
        def store(at, value):
            part[n, :, at] = value.astype(BF16)

        return store

    def into_keep(n):
        def store(at, value):
            keep[n, :, at] = value

        return store

    b_left0 = remote(part.at[0], back.at[2], bs_sem.at[0], br_sem.at[0], left)
    b_right1 = remote(part.at[1], back.at[1], bs_sem.at[1], br_sem.at[1], right)
    b_across0 = remote(part.at[2], stage.at[0], bs_sem.at[2], br_sem.at[2], right)
    b_across1 = remote(part.at[3], stage.at[1], bs_sem.at[3], br_sem.at[3], left)
    b_right0 = remote(part.at[4], back.at[0], bs_sem.at[4], br_sem.at[4], right)
    b_left1 = remote(part.at[5], back.at[3], bs_sem.at[5], br_sem.at[5], left)

    unpack(0)
    zc["r", 0].start()
    zc["l", 0].start()
    unpack(1)
    zc["l", 1].start()
    zc["r", 1].start()
    expert(0, 0, into_own(0))
    zc["r", 0].wait_recv()
    zc["ro"].start()
    expert(0, 1, into_own(1))
    zc["l", 1].wait_recv()
    zc["lo"].start()
    expert(1, 0, into_part(0))
    b_left0.start()
    zc["r", 1].wait_recv()
    expert(1, 1, into_keep(1))
    expert(2, 1, into_part(1))
    b_right1.start()
    zc["l", 0].wait_recv()
    expert(2, 0, into_keep(0))
    zc["ro"].wait_recv()
    expert(3, 0, into_part(2))
    b_across0.start()
    zc["lo"].wait_recv()
    expert(3, 1, into_part(3))
    b_across1.start()
    b_across0.wait_recv()
    part[4] = (keep[0] + stage[0].astype(F32)).astype(BF16)
    b_right0.start()
    b_across1.wait_recv()
    part[5] = (keep[1] + stage[1].astype(F32)).astype(BF16)
    b_left1.start()

    b_left0.wait_recv()
    b_right1.wait_recv()
    for half in range(2):
        if half == 0:
            b_right0.wait_recv()
        else:
            b_left1.wait_recv()
        for cc in range(NC):
            at = slice(cc * COL, (cc + 1) * COL)
            full = own[half, :, at] + back[half, :, at].astype(F32) + back[2 + half, :, at].astype(F32)
            rst[pl.ds(cc * CR, CR), :] = full.astype(BF16)
        packed = dot(pkm[0], rst[pl.ds(0, CR), :])
        for cc in range(1, NC):
            packed += dot(pkm[cc], rst[pl.ds(cc * CR, CR), :])
        pack[pl.ds(half * HALF * MSG, HALF * MSG), :] = packed.astype(BF16)

        def to_patch(j, _):
            dest = shifted(j, -1)
            remote(pack.at[rows48(j), :], ret.at[rows48(d), :], es_sem, er_sem, (dest, z)).start()
            return 0

        lax.fori_loop(max(1, half * HALF), (half + 1) * HALF, to_patch, 0)
    ret[rows48(d), :] = pack[pl.ds(0, MSG), :]

    others = ret.at[pl.ds(0, (NE - 1) * MSG), :]
    remote(others, others, es_sem, er_sem, right).wait_recv()
    g0, g1 = gcol[:, 2:3], gcol[:, 3:4]

    def final(cc, _):
        both = dot(pick[pl.ds(pl.multiple_of(cc * 256, 256), 256), :], ret[...])
        out[:, cols(cc)] = (mid[:, cols(cc)] + g0 * both[:TOK] + g1 * both[TOK:]).astype(BF16)
        return 0

    lax.fori_loop(0, NC, final, 0)

    for copy in seg_copies + [r0, r1, l0, l1, ro, lo] + list(zc.values()):
        copy.wait_send()
    for copy in (b_left0, b_right1, b_across0, b_across1, b_right0, b_left1):
        copy.wait_send()
    gone = send.at[pl.ds(0, (NE - 1) * MSG), :]
    remote(gone, gone, ds_sem, dr_sem.at[0], right).wait_send()
    gone = pack.at[pl.ds(0, (NE - 1) * MSG), :]
    remote(gone, gone, es_sem, er_sem, right).wait_send()


def layer(tok, seg, eid, gate, lna, lne, wqkv, wao, win, wout):
    vm = pl.BlockSpec(memory_space=pltpu.VMEM)
    hbm = pl.BlockSpec(memory_space=pl.ANY)
    V = pltpu.VMEM
    dma = pltpu.SemaphoreType.DMA
    return pl.pallas_call(
        kernel,
        out_shape=jax.ShapeDtypeStruct((TOK, D), BF16),
        in_specs=[vm] * 6 + [hbm] * 4,
        out_specs=vm,
        scratch_shapes=[
            V((D, 3 * D), BF16),
            V((D, D), BF16),
            V((D, D), BF16),
            V((D, D), BF16),
            V((4 * TOK, D), BF16),
            V((4, 8, TOK), I32),
            V((TOK, D), BF16),
            V((4 * TOK, D), BF16),
            V((4 * TOK, D), BF16),
            V((TOK, D), F32),
            V((TOK, D), BF16),
            V((TOK, D), F32),
            V((NC * TOK, COL), BF16),
            V((ALL, NC * TOK), BF16),
            V((ALL, COL), BF16),
            V((ALL, COL), BF16),
            V((4, 2, CR, D), BF16),
            V((CR, D), BF16),
            V((6, CR, D), BF16),
            V((2, CR, D), F32),
            V((2, CR, D), F32),
            V((2, CR, D), BF16),
            V((4, CR, D), BF16),
            V((NC * CR, COL), BF16),
            V((ALL, COL), BF16),
            V((ALL, COL), BF16),
            V((2 * NC * TOK, ALL), BF16),
            V((NC * CR, HALF * MSG), BF16),
            V((NC, HALF * MSG, CR), BF16),
            V((TOK, TOK), F32),
            dma((6,)),
            dma((6,)),
            dma((6,)),
            dma((3,)),
            dma((3,)),
            dma,
            dma((2,)),
            dma((6,)),
            dma((6,)),
            dma((6,)),
            dma((6,)),
            dma,
            dma,
        ],
        compiler_params=pltpu.CompilerParams(
            collective_id=0, has_side_effects=True, vmem_limit_bytes=60 * 1024 * 1024
        ),
        cost_estimate=pl.CostEstimate(
            flops=14_000_000_000, bytes_accessed=24_000_000, transcendentals=3_000_000
        ),
    )(tok, seg, eid, gate, lna, lne, wqkv, wao, win, wout)


def body(
    tokens, segment_ids, expert_ids, gate_values, ln_attn, w_qkv, w_attn_out, ln_expert, w_in, w_out
):
    out = layer(
        tokens[0],
        segment_ids,
        expert_ids[0].T,
        gate_values[0].T,
        ln_attn[None],
        ln_expert[None],
        w_qkv,
        w_attn_out,
        w_in[0],
        w_out[0],
    )
    return out[None]


def solution(mesh):
    placed = (
        P("dp", "seq", None),
        P("dp", "seq"),
        P("dp", "seq", None),
        P("dp", "seq", None),
        P(),
        P(),
        P(),
        P(),
        P("dp", None, "seq"),
        P("dp", "seq", None),
    )
    return jax.shard_map(
        body, mesh=mesh, in_specs=placed, out_specs=P("dp", "seq", None), check_vma=False
    )
```

time: 290 us -> 114 us (0.39)
  Pallas kernels: 0 us -> 110 us
  waiting for transfers between devices: 97.6 us -> 0 us
  blocking collectives: 84.1 us -> 0 us
  local copies, waits for them, and re-layouts: 46.3 us -> 4.3 us
  matrix products: 29.4 us -> 0 us
  between operations: 13.6 us -> 0.01 us
  other arithmetic: 13.3 us -> 0 us
  starting transfers between devices: 5.13 us -> 0 us
    pallas_call x0 -> x1, Pallas kernels: none -> 110 us  [layer(): pl.pallas_call(kernel, out_shape=jax.ShapeDtypeStruct((TOK, D), BF16), in...]
    all_to_all x1 -> x0, blocking collectives: 74.3 us -> none  [body(): lax.all_to_all(copies, ('dp', 'seq'), split_axis=0, concat_axis=0, tiled=...]
    all_to_all x1 -> x0, waiting for transfers between devices: 64.5 us -> none  [body(): lax.all_to_all(partial_value.astype(jnp.bfloat16), ('dp', 'seq'), split_a...]
    all_gather x2 -> x0, waiting for transfers between devices: 32.4 us -> none  [the longest x1 19.2 us: body(): values = lax.all_gather(own_values, 'seq', axis=0, tiled=True)]
    dot_general x6 -> x0, matrix products: 29.4 us -> none  [the longest x1 8.54 us: expert_rows(): return jnp.dot(hidden, second, preferred_element_type=jnp.float32)]
    reduce_sum x7 -> x0, other arithmetic: 10.5 us -> none  [the longest x1 3.44 us: body(): jnp.sum(coming.reshape(experts, groups, capacity, width), axis=1)]
    all_gather x1 -> x0, blocking collectives: 9.76 us -> none  [body(): key_seg = lax.all_gather(query_seg, 'seq', axis=0, tiled=True)]
    reshape x2 -> x0, local copies, waits for them, and re-layouts: 8.71 us -> none  [the longest x1 5.99 us: body(): arrived.reshape(-1, width)]
  transfers between devices with their start and end apart: 3 -> 0, of which waited for: 3 -> 0; matrix products, arithmetic and copies ran while one was open for 3% -> 0% of each run, Pallas kernels for 0% -> 0%
where the time goes in v1:
time: 114 us
  Pallas kernels  110 us (96%)
  local copies, waits for them, and re-layouts  4.3 us (4%)
    pallas_call x1, Pallas kernels, layer(): pl.pallas_call(kernel, out_shape=jax.ShapeDtypeStruct((TOK, D), BF16), in...  110 us

profile of v1, /device:TPU:1, one launch (start us, length us, event | category | flops | bytes accessed | tf_op | source)
XLA Modules:
  0.0 113.9 jit_solution(5929524430093226531)
XLA Ops:
  0.0 1.3 %broadcast_in_dim.9.lna = f32[1,1280]{1,0:T(1,128)} reshape(f32[1280]{0:T(1024)} %param.14) | data formatting | bytes 10240 | tf_op jit(solution)/shard_map/broadcast_in_dim | solution.py:485
  1.3 1.3 %broadcast_in_dim.10.lne = f32[1,1280]{1,0:T(1,128)} reshape(f32[1280]{0:T(1024)} %param.17) | data formatting | bytes 10240 | tf_op jit(solution)/shard_map/broadcast_in_dim | solution.py:486
  2.6 109.6 %shard_map.100 = bf16[128,1280]{1,0:T(8,128)(2,1)} custom-call(bf16[128,1280]{1,0:T(8,128)(2,1)} %bitcast.13, s32[1,128]{1,0:T(1,128)} %seg.1, s32[2,128]{1,0:T(2,128)} %bitcast.14, f32[2,128]{1,0:T(2,128)} %bitcast.15, f32[1,1280]{1,0:T(1,128)} %broadcast_in_dim.9.lna, f32[1,1280]{1,0:T(1,128)} %broadcast_in_dim.10.lne, bf16[1280,3840]{1,0:T(8,128)(2,1)} %wqkv_h.1, ...), custom_call_target="tpu_custom_call" | custom-call | flops 14000000000 | bytes 24000000 | tf_op jit(solution)/shard_map/pallas_call | solution.py:418
  112.2 1.7 %copy.12 = bf16[1,128,1280]{2,1,0:T(8,128)(2,1)} copy(bf16[1,128,1280]{2,1,0:T(8,128)(2,1)} %bitcast.10) | data formatting | bytes 655360

commit v2 on v1

--- a/solution.py
+++ b/solution.py
@@ -23,11 +23,22 @@
 MSG = 48
 HALF = 16
 CR = HALF * CAP
+GS = 8
+GM = GS * MSG
 ALL = NE * MSG
 EPS = 1e-06
 NEG = -1e30
 
 GROUPS = (((0, 1, 2), 0), ((3,), 128), ((4, 5), 256), ((6, 7), 384))
+
+
+OFFSETS = sorted(
+    [(dx, dy, dc) for dx in range(4) for dy in range(4) for dc in range(2)],
+    key=lambda o: -(min(o[0], 4 - o[0]) + min(o[1], 4 - o[1]) + 0.5 * o[2]),
+)
+
+OUT = ((0, 64), (64, 80))
+BACK = ((0, 80), (80, 64))
 
 
 def normalize(rows, gain):
@@ -56,7 +67,7 @@
 def kernel(
     tok, seg, eid, gate, lna, lne, wqkv_h, wao_h, win_h, wout_h, out,
     wqkv, wao, win, wout, xn, segs, q, k, v, ctx, ctxb, mid, xp, g, send, rcv, a, hid,
-    part, keep, own, stage, back, rst, pack, ret, pick, unp, pkm, gcol,
+    part, keep, own, stage, back, rst, pack, ret, pick, unp0, unp1, pkm0, pkm1, gcol,
     w_sem, as_sem, ar_sem, ss_sem, sr_sem, ds_sem, dr_sem, zs_sem, zr_sem, bs_sem, br_sem,
     es_sem, er_sem,
 ):
@@ -67,11 +78,13 @@
     zo = lax.rem(z + 2, 4)
     x, y, c = d // 8, lax.rem(d // 2, 4), lax.rem(d, 2)
 
-    def shifted(j, sign):
-        dx, dy, dc = j // 8, lax.rem(j // 2, 4), lax.rem(j, 2)
-        if sign < 0:
-            dx, dy = 4 - dx, 4 - dy
-        return lax.rem(x + dx, 4) * 8 + lax.rem(y + dy, 4) * 2 + lax.rem(c + dc, 2)
+    xs = [lax.rem(x + i, 4) * 8 for i in range(4)]
+    ys = [lax.rem(y + i, 4) * 2 for i in range(4)]
+    cs = [c, 1 - c]
+
+    def shifted(n, sign):
+        dx, dy, dc = OFFSETS[n]
+        return xs[sign * dx % 4] + ys[sign * dy % 4] + cs[dc]
 
     def rows48(j):
         return pl.ds(pl.multiple_of(j * MSG, MSG), MSG)
@@ -83,19 +96,16 @@
     loads.append(pltpu.make_async_copy(wao_h, wao, w_sem.at[3]))
     loads.append(pltpu.make_async_copy(win_h, win, w_sem.at[4]))
     loads.append(pltpu.make_async_copy(wout_h, wout, w_sem.at[5]))
-    for load in loads:
+    for load in loads[:3]:
         load.start()
 
     barrier = pltpu.get_barrier_semaphore()
     for other in (zl, zr, zo):
         pl.semaphore_signal(barrier, inc=1, device_id=(d, other), device_id_type=MESH)
 
-    def greet(j, _):
-        pl.semaphore_signal(barrier, inc=1, device_id=(shifted(j, 1), z), device_id_type=MESH)
-        return 0
-
-    lax.fori_loop(1, NE, greet, 0)
-    xn[pl.ds(0, TOK), :] = normalize(tok[...].astype(F32), lna[...]).astype(BF16)
+    for n in range(NE - 1):
+        pl.semaphore_signal(barrier, inc=1, device_id=(shifted(n, 1), z), device_id_type=MESH)
+    xn[pl.ds(0, TOK), :] = normalize(tok[...].astype(F32), lna[...].reshape(1, D)).astype(BF16)
     segs[0] = jnp.broadcast_to(seg[...], (8, TOK))
     pl.semaphore_wait(barrier, NE - 1 + 3)
 
@@ -127,6 +137,8 @@
     l0.start()
     for copy in seg_copies:
         copy.start()
+    for load in loads[3:]:
+        load.start()
 
     e0, e1 = eid[0:1, :], eid[1:2, :]
     ei = iota((NE, TOK), 0)
@@ -154,6 +166,25 @@
 
     lax.fori_loop(0, ALL // 256, make_g, 0)
 
+    def fixed(ref, q_dim, rows, first, base):
+        q = iota(ref.shape, q_dim)
+        r = iota(ref.shape, 1 - q_dim) + base
+        if rows == 64:
+            cc = lax.shift_right_logical(q, 6)
+        else:
+            cc = lax.shift_right_logical(q * 205, 14)
+        i = q - cc * rows + first
+        at = i + (MSG - CAP) * lax.shift_right_logical(i * 57, 9) + CAP * cc
+        ref[...] = jnp.where(r == at, 1.0, 0.0).astype(BF16)
+
+    fixed(unp0, 0, 64, 0, 0)
+    fixed(unp1, 0, 80, 64, 7 * MSG)
+
+    r0.wait_recv()
+    ro.start()
+    l1.wait_recv()
+    lo.start()
+
     for load in loads[:3]:
         load.wait()
 
@@ -174,21 +205,8 @@
         lax.fori_loop(0, NC, step, 0)
 
     keys_values(0, TOK)
-    r0.wait_recv()
-    ro.start()
-    l1.wait_recv()
-    lo.start()
-
-    i = iota((CR, HALF * MSG), 0)
-    r = iota((CR, HALF * MSG), 1)
-    at = i + (MSG - CAP) * lax.shift_right_logical(i * 57, 9)
-    for cc in range(NC):
-        unp[pl.ds(cc * CR, CR), :] = jnp.where(r == at + CAP * cc, 1.0, 0.0).astype(BF16)
-    i = iota((HALF * MSG, CR), 1)
-    r = iota((HALF * MSG, CR), 0)
-    at = i + (MSG - CAP) * lax.shift_right_logical(i * 57, 9)
-    for cc in range(NC):
-        pkm[cc] = jnp.where(r == at + CAP * cc, 1.0, 0.0).astype(BF16)
+    fixed(pkm0, 1, 80, 0, 0)
+    fixed(pkm1, 1, 80, 64, GM)
 
     r1.wait_recv()
     l0.wait_recv()
@@ -250,7 +268,7 @@
         return 0
 
     lax.fori_loop(0, NC, project, 0)
-    expert_in = normalize(mid[...], lne[...]).astype(BF16)
+    expert_in = normalize(mid[...], lne[...].reshape(1, D)).astype(BF16)
     for cc in range(NC):
         xp[pl.ds(cc * TOK, TOK), :] = expert_in[:, cc * COL : (cc + 1) * COL]
 
@@ -261,38 +279,52 @@
 
     lax.fori_loop(0, ALL // 256, fill, 0)
 
-    def to_expert(j, _):
-        dest = shifted(j, 1)
+    for n in range(NE - 1):
+        dest = shifted(n, 1)
         remote(
-            send.at[rows48(dest), :], rcv.at[rows48(j), :], ds_sem, dr_sem.at[j // HALF], (dest, z)
+            send.at[rows48(dest), :], rcv.at[rows48(n), :], ds_sem, dr_sem.at[n // GS], (dest, z)
         ).start()
-        return 0
-
-    lax.fori_loop(1, NE, to_expert, 0)
-    rcv[pl.ds(0, MSG), :] = send[rows48(d), :]
-
-    loads[4].wait()
-    loads[5].wait()
-
-    def chunk(slot, half):
-        return a.at[slot, half]
-
-    def unpack(half):
-        first, number = (MSG, (HALF - 1) * MSG) if half == 0 else (HALF * MSG, HALF * MSG)
-        got = rcv.at[pl.ds(first, number), :]
-        remote(got, got, ds_sem, dr_sem.at[half], right).wait_recv()
+    rcv[pl.ds((NE - 1) * MSG, MSG), :] = send[rows48(d), :]
+
+    def piece_of(slot, half, n):
+        first, number = OUT[n]
+        return a.at[slot, half, pl.ds(first, number)]
+
+    def arrived(group):
+        number = GS if group < 3 else GS - 1
+        got = rcv.at[pl.ds(group * GM, number * MSG), :]
+        remote(got, got, ds_sem, dr_sem.at[group], right).wait_recv()
+
+    def unpack(half, n):
+        first, number = OUT[n]
+        arrived(2 * half + n)
+        base = half * 2 * GM
+        if n == 0:
+            got = dot(unp0[...], rcv[pl.ds(base, GM), :])
+        else:
+            got = dot(unp1[...], rcv[pl.ds(base + 7 * MSG, 9 * MSG), :])
         for cc in range(NC):
-            piece = dot(unp[pl.ds(cc * CR, CR), :], rcv[pl.ds(half * HALF * MSG, HALF * MSG), :])
-            a[0, half, :, cc * COL : (cc + 1) * COL] = piece.astype(BF16)
+            a[0, half, first : first + number, cc * COL : (cc + 1) * COL] = got[
+                cc * number : (cc + 1) * number
+            ].astype(BF16)
 
     zc = {}
     for half in range(2):
-        zc["r", half] = remote(chunk(0, half), chunk(1, half), zs_sem.at[half], zr_sem.at[half], right)
-        zc["l", half] = remote(
-            chunk(0, half), chunk(2, half), zs_sem.at[2 + half], zr_sem.at[2 + half], left
+        for n in range(2):
+            m = 2 * half + n
+            zc["r", half, n] = remote(
+                piece_of(0, half, n), piece_of(1, half, n), zs_sem.at[m], zr_sem.at[m], right
+            )
+            zc["l", half, n] = remote(
+                piece_of(0, half, n), piece_of(2, half, n), zs_sem.at[4 + m], zr_sem.at[4 + m], left
+            )
+    for n in range(2):
+        zc["ro", n] = remote(
+            piece_of(1, 0, n), piece_of(3, 0, n), zs_sem.at[8 + n], zr_sem.at[8 + n], right
         )
-    zc["ro"] = remote(chunk(1, 0), chunk(3, 0), zs_sem.at[4], zr_sem.at[4], right)
-    zc["lo"] = remote(chunk(2, 1), chunk(3, 1), zs_sem.at[5], zr_sem.at[5], left)
+        zc["lo", n] = remote(
+            piece_of(2, 1, n), piece_of(3, 1, n), zs_sem.at[10 + n], zr_sem.at[10 + n], left
+        )
 
     def expert(slot, half, store):
         def first(j, _):
@@ -325,69 +357,100 @@
 
         return store
 
+    def back_of(ref, slot, n):
+        first, number = BACK[n]
+        return ref.at[slot, pl.ds(first, number)]
+
     b_left0 = remote(part.at[0], back.at[2], bs_sem.at[0], br_sem.at[0], left)
     b_right1 = remote(part.at[1], back.at[1], bs_sem.at[1], br_sem.at[1], right)
-    b_across0 = remote(part.at[2], stage.at[0], bs_sem.at[2], br_sem.at[2], right)
-    b_across1 = remote(part.at[3], stage.at[1], bs_sem.at[3], br_sem.at[3], left)
-    b_right0 = remote(part.at[4], back.at[0], bs_sem.at[4], br_sem.at[4], right)
-    b_left1 = remote(part.at[5], back.at[3], bs_sem.at[5], br_sem.at[5], left)
-
-    unpack(0)
-    zc["r", 0].start()
-    zc["l", 0].start()
-    unpack(1)
-    zc["l", 1].start()
-    zc["r", 1].start()
+    bc = {}
+    for n in range(2):
+        for m, (key, src, dst, at, dev) in enumerate(
+            (
+                ("across0", 2, stage, 0, right),
+                ("across1", 3, stage, 1, left),
+                ("right0", 4, back, 0, right),
+                ("left1", 5, back, 3, left),
+            )
+        ):
+            bc[key, n] = remote(
+                back_of(part, src, n), back_of(dst, at, n),
+                bs_sem.at[2 + 2 * m + n], br_sem.at[2 + 2 * m + n], dev,
+            )
+
+    loads[4].wait()
+    loads[5].wait()
+
+    for half in range(2):
+        for n in range(2):
+            unpack(half, n)
+            zc["r", half, n].start()
+            zc["l", half, n].start()
+    for n in range(2):
+        zc["r", 0, n].wait_recv()
+        zc["ro", n].start()
     expert(0, 0, into_own(0))
-    zc["r", 0].wait_recv()
-    zc["ro"].start()
-    expert(0, 1, into_own(1))
-    zc["l", 1].wait_recv()
-    zc["lo"].start()
+    for n in range(2):
+        zc["l", 1, n].wait_recv()
+        zc["lo", n].start()
     expert(1, 0, into_part(0))
     b_left0.start()
-    zc["r", 1].wait_recv()
-    expert(1, 1, into_keep(1))
     expert(2, 1, into_part(1))
     b_right1.start()
-    zc["l", 0].wait_recv()
+    for n in range(2):
+        zc["r", 1, n].wait_recv()
+        zc["l", 0, n].wait_recv()
     expert(2, 0, into_keep(0))
-    zc["ro"].wait_recv()
+    expert(1, 1, into_keep(1))
+    expert(0, 1, into_own(1))
+    for n in range(2):
+        zc["ro", n].wait_recv()
     expert(3, 0, into_part(2))
-    b_across0.start()
-    zc["lo"].wait_recv()
+    bc["across0", 0].start()
+    bc["across0", 1].start()
+    for n in range(2):
+        zc["lo", n].wait_recv()
     expert(3, 1, into_part(3))
-    b_across1.start()
-    b_across0.wait_recv()
-    part[4] = (keep[0] + stage[0].astype(F32)).astype(BF16)
-    b_right0.start()
-    b_across1.wait_recv()
-    part[5] = (keep[1] + stage[1].astype(F32)).astype(BF16)
-    b_left1.start()
+    bc["across1", 0].start()
+    bc["across1", 1].start()
+    for n in range(2):
+        first, number = BACK[n]
+        rows = pl.ds(first, number)
+        bc["across0", n].wait_recv()
+        part[4, rows] = (keep[0, rows] + stage[0, rows].astype(F32)).astype(BF16)
+        bc["right0", n].start()
+        bc["across1", n].wait_recv()
+        part[5, rows] = (keep[1, rows] + stage[1, rows].astype(F32)).astype(BF16)
+        bc["left1", n].start()
 
     b_left0.wait_recv()
     b_right1.wait_recv()
-    for half in range(2):
-        if half == 0:
-            b_right0.wait_recv()
-        else:
-            b_left1.wait_recv()
-        for cc in range(NC):
-            at = slice(cc * COL, (cc + 1) * COL)
-            full = own[half, :, at] + back[half, :, at].astype(F32) + back[2 + half, :, at].astype(F32)
-            rst[pl.ds(cc * CR, CR), :] = full.astype(BF16)
-        packed = dot(pkm[0], rst[pl.ds(0, CR), :])
-        for cc in range(1, NC):
-            packed += dot(pkm[cc], rst[pl.ds(cc * CR, CR), :])
-        pack[pl.ds(half * HALF * MSG, HALF * MSG), :] = packed.astype(BF16)
-
-        def to_patch(j, _):
-            dest = shifted(j, -1)
-            remote(pack.at[rows48(j), :], ret.at[rows48(d), :], es_sem, er_sem, (dest, z)).start()
-            return 0
-
-        lax.fori_loop(max(1, half * HALF), (half + 1) * HALF, to_patch, 0)
-    ret[rows48(d), :] = pack[pl.ds(0, MSG), :]
+    for n in range(2):
+        first, number = BACK[n]
+        rows = pl.ds(first, number)
+        for half in range(2):
+            bc["right0" if half == 0 else "left1", n].wait_recv()
+            for cc in range(NC):
+                at = slice(cc * COL, (cc + 1) * COL)
+                full = (
+                    own[half, rows, at]
+                    + back[half, rows, at].astype(F32)
+                    + back[2 + half, rows, at].astype(F32)
+                ).astype(BF16)
+                if n == 0:
+                    rst[half, 0, pl.ds(cc * 80, 80), :] = full
+                    rst[half, 1, pl.ds(cc * 80, 16), :] = full[64:]
+                else:
+                    rst[half, 1, pl.ds(cc * 80 + 16, 64), :] = full
+            packed = dot((pkm0 if n == 0 else pkm1)[...], rst[half, n])
+            group = 2 * half + n
+            pack[pl.ds(group * GM, GM), :] = packed.astype(BF16)
+            for m in range(group * GS, min((group + 1) * GS, NE - 1)):
+                dest = shifted(m, -1)
+                remote(
+                    pack.at[rows48(m), :], ret.at[rows48(d), :], es_sem, er_sem, (dest, z)
+                ).start()
+    ret[rows48(d), :] = pack[pl.ds((NE - 1) * MSG, MSG), :]
 
     others = ret.at[pl.ds(0, (NE - 1) * MSG), :]
     remote(others, others, es_sem, er_sem, right).wait_recv()
@@ -402,7 +465,7 @@
 
     for copy in seg_copies + [r0, r1, l0, l1, ro, lo] + list(zc.values()):
         copy.wait_send()
-    for copy in (b_left0, b_right1, b_across0, b_across1, b_right0, b_left1):
+    for copy in [b_left0, b_right1] + list(bc.values()):
         copy.wait_send()
     gone = send.at[pl.ds(0, (NE - 1) * MSG), :]
     remote(gone, gone, ds_sem, dr_sem.at[0], right).wait_send()
@@ -444,12 +507,14 @@
             V((2, CR, D), F32),
             V((2, CR, D), BF16),
             V((4, CR, D), BF16),
-            V((NC * CR, COL), BF16),
+            V((2, 2, NC * 80, COL), BF16),
             V((ALL, COL), BF16),
             V((ALL, COL), BF16),
             V((2 * NC * TOK, ALL), BF16),
-            V((NC * CR, HALF * MSG), BF16),
-            V((NC, HALF * MSG, CR), BF16),
+            V((NC * 64, GM), BF16),
+            V((NC * 80, 9 * MSG), BF16),
+            V((GM, NC * 80), BF16),
+            V((GM, NC * 80), BF16),
             V((TOK, TOK), F32),
             dma((6,)),
             dma((6,)),
@@ -457,11 +522,11 @@
             dma((3,)),
             dma((3,)),
             dma,
-            dma((2,)),
-            dma((6,)),
-            dma((6,)),
-            dma((6,)),
-            dma((6,)),
+            dma((4,)),
+            dma((12,)),
+            dma((12,)),
+            dma((10,)),
+            dma((10,)),
             dma,
             dma,
         ],
@@ -482,8 +547,8 @@
         segment_ids,
         expert_ids[0].T,
         gate_values[0].T,
-        ln_attn[None],
-        ln_expert[None],
+        ln_attn,
+        ln_expert,
         w_qkv,
         w_attn_out,
         w_in[0],

time: 114 us -> 104 us (0.912)
  Pallas kernels: 110 us -> 102 us
  local copies, waits for them, and re-layouts: 4.3 us -> 1.72 us
    pallas_call x1, Pallas kernels: 110 us -> 102 us  [layer(): pl.pallas_call(kernel, out_shape=jax.ShapeDtypeStruct((TOK, D), BF16), in...]
    broadcast_in_dim x2 -> x0, local copies, waits for them, and re-layouts: 2.58 us -> none  [the longest x1 1.29 us: body(): ln_attn[None]]
where the time goes in v2:
time: 104 us
  Pallas kernels  102 us (98%)
  local copies, waits for them, and re-layouts  1.72 us (2%)
    pallas_call x1, Pallas kernels, layer(): pl.pallas_call(kernel, out_shape=jax.ShapeDtypeStruct((TOK, D), BF16), in...  102 us

profile of v2, /device:TPU:1, one launch (start us, length us, event | category | flops | bytes accessed | tf_op | source)
XLA Modules:
  0.0 103.8 jit_solution(6152168129850587771)
XLA Ops:
  0.0 102.1 %shard_map.100 = bf16[128,1280]{1,0:T(8,128)(2,1)} custom-call(bf16[128,1280]{1,0:T(8,128)(2,1)} %bitcast.13, s32[1,128]{1,0:T(1,128)} %seg.1, s32[2,128]{1,0:T(2,128)} %bitcast.14, f32[2,128]{1,0:T(2,128)} %bitcast.15, f32[1280]{0:T(1024)} %lna.1, f32[1280]{0:T(1024)} %lne.1, bf16[1280,3840]{1,0:T(8,128)(2,1)} %wqkv_h.1, bf16[1280,1280]{1,0:T(8,128)(2,1)} %wao_h.1, ...), custom_call_target="tpu_custom_call" | custom-call | flops 14000000000 | bytes 24000000 | tf_op jit(solution)/shard_map/pallas_call | solution.py:481
  102.1 1.7 %copy.12 = bf16[1,128,1280]{2,1,0:T(8,128)(2,1)} copy(bf16[1,128,1280]{2,1,0:T(8,128)(2,1)} %bitcast.10) | data formatting | bytes 655360

commit v3 on v2

--- a/solution.py
+++ b/solution.py
@@ -61,7 +61,12 @@
 
 
 def cols(j):
-    return pl.ds(pl.multiple_of(j * COL, COL), COL)
+    return pl.ds(j * COL, COL)
+
+
+def each(number, step):
+    for i in range(number):
+        step(i)
 
 
 def kernel(
@@ -156,15 +161,14 @@
     gcol[...] = jnp.transpose(square)
     t0, t1 = t0.astype(I32), t1.astype(I32)
 
-    def make_g(i, _):
-        rows = pl.ds(pl.multiple_of(i * 256, 256), 256)
+    def make_g(i):
+        rows = pl.ds(i * 256, 256)
         r = iota((256, TOK), 0) + i * 256
         for cc in range(NC):
             hit = (r == t0 + CAP * cc) | (r == t1 + CAP * cc)
             g[rows, cc * TOK : (cc + 1) * TOK] = jnp.where(hit, 1.0, 0.0).astype(BF16)
-        return 0
-
-    lax.fori_loop(0, ALL // 256, make_g, 0)
+
+    each(ALL // 256, make_g)
 
     def fixed(ref, q_dim, rows, first, base):
         q = iota(ref.shape, q_dim)
@@ -188,21 +192,19 @@
     for load in loads[:3]:
         load.wait()
 
-    def own_q(j, _):
+    def own_q(j):
         q[:, cols(j)] = dot(xn[pl.ds(0, TOK), :], wqkv[:, cols(j)]).astype(BF16)
-        return 0
-
-    lax.fori_loop(0, NC, own_q, 0)
+
+    each(NC, own_q)
 
     def keys_values(first, number):
         rows = pl.ds(first, number)
 
-        def step(j, _):
+        def step(j):
             k[rows, cols(j)] = dot(xn[rows, :], wqkv[:, cols(j + NC)]).astype(BF16)
             v[rows, cols(j)] = dot(xn[rows, :], wqkv[:, cols(j + 2 * NC)]).astype(BF16)
-            return 0
-
-        lax.fori_loop(0, NC, step, 0)
+
+        each(NC, step)
 
     keys_values(0, TOK)
     fixed(pkm0, 1, 80, 0, 0)
@@ -215,13 +217,12 @@
     ri = iota((TOK, ALL), 1)
     c0, c1 = gcol[:, 0:1].astype(I32), gcol[:, 1:2].astype(I32)
 
-    def make_pick(cc, _):
-        base = pl.multiple_of(cc * 256, 256)
+    def make_pick(cc):
+        base = cc * 256
         pick[pl.ds(base, TOK), :] = jnp.where(ri == c0 + CAP * cc, 1.0, 0.0).astype(BF16)
         pick[pl.ds(base + TOK, TOK), :] = jnp.where(ri == c1 + CAP * cc, 1.0, 0.0).astype(BF16)
-        return 0
-
-    lax.fori_loop(0, NC, make_pick, 0)
+
+    each(NC, make_pick)
 
     for copy in seg_copies:
         copy.wait_recv()
@@ -263,21 +264,19 @@
 
     loads[3].wait()
 
-    def project(j, _):
+    def project(j):
         mid[:, cols(j)] = tok[:, cols(j)].astype(F32) + dot(ctxb[...], wao[:, cols(j)])
-        return 0
-
-    lax.fori_loop(0, NC, project, 0)
+
+    each(NC, project)
     expert_in = normalize(mid[...], lne[...].reshape(1, D)).astype(BF16)
     for cc in range(NC):
         xp[pl.ds(cc * TOK, TOK), :] = expert_in[:, cc * COL : (cc + 1) * COL]
 
-    def fill(i, _):
-        rows = pl.ds(pl.multiple_of(i * 256, 256), 256)
+    def fill(i):
+        rows = pl.ds(i * 256, 256)
         send[rows, :] = dot(g[rows, :], xp[...]).astype(BF16)
-        return 0
-
-    lax.fori_loop(0, ALL // 256, fill, 0)
+
+    each(ALL // 256, fill)
 
     for n in range(NE - 1):
         dest = shifted(n, 1)
@@ -327,17 +326,15 @@
         )
 
     def expert(slot, half, store):
-        def first(j, _):
+        def first(j):
             hid[:, cols(j)] = gelu(dot(a[slot, half], win[:, cols(j)])).astype(BF16)
-            return 0
-
-        lax.fori_loop(0, NC, first, 0)
-
-        def second(j, _):
+
+        each(NC, first)
+
+        def second(j):
             store(cols(j), dot(hid[...], wout[:, cols(j)]))
-            return 0
-
-        lax.fori_loop(0, NC, second, 0)
+
+        each(NC, second)
 
     def into_own(half):
         def store(at, value):
@@ -456,12 +453,11 @@
     remote(others, others, es_sem, er_sem, right).wait_recv()
     g0, g1 = gcol[:, 2:3], gcol[:, 3:4]
 
-    def final(cc, _):
-        both = dot(pick[pl.ds(pl.multiple_of(cc * 256, 256), 256), :], ret[...])
+    def final(cc):
+        both = dot(pick[pl.ds(cc * 256, 256), :], ret[...])
         out[:, cols(cc)] = (mid[:, cols(cc)] + g0 * both[:TOK] + g1 * both[TOK:]).astype(BF16)
-        return 0
-
-    lax.fori_loop(0, NC, final, 0)
+
+    each(NC, final)
 
     for copy in seg_copies + [r0, r1, l0, l1, ro, lo] + list(zc.values()):
         copy.wait_send()

time: 104 us -> 96.8 us (0.931)
  Pallas kernels: 102 us -> 94.9 us
    pallas_call x1, Pallas kernels: 102 us -> 94.9 us  [layer(): pl.pallas_call(kernel, out_shape=jax.ShapeDtypeStruct((TOK, D), BF16), in...]
where the time goes in v3:
time: 96.8 us; the launch traced here: 96.6 us
  Pallas kernels  94.9 us (98%)
  local copies, waits for them, and re-layouts  1.72 us (2%)
    pallas_call x1, Pallas kernels, layer(): pl.pallas_call(kernel, out_shape=jax.ShapeDtypeStruct((TOK, D), BF16), in...  94.9 us

profile of v3, /device:TPU:1, one launch (start us, length us, event | category | flops | bytes accessed | tf_op | source)
XLA Modules:
  0.0 96.6 jit_solution(8281061907707959269)
XLA Ops:
  0.0 94.9 %shard_map.100 = bf16[128,1280]{1,0:T(8,128)(2,1)} custom-call(bf16[128,1280]{1,0:T(8,128)(2,1)} %bitcast.13, s32[1,128]{1,0:T(1,128)} %seg.1, s32[2,128]{1,0:T(2,128)} %bitcast.14, f32[2,128]{1,0:T(2,128)} %bitcast.15, f32[1280]{0:T(1024)} %lna.1, f32[1280]{0:T(1024)} %lne.1, bf16[1280,3840]{1,0:T(8,128)(2,1)} %wqkv_h.1, bf16[1280,1280]{1,0:T(8,128)(2,1)} %wao_h.1, ...), custom_call_target="tpu_custom_call" | custom-call | flops 14000000000 | bytes 24000000 | tf_op jit(solution)/shard_map/pallas_call | solution.py:477
  94.9 1.7 %copy.12 = bf16[1,128,1280]{2,1,0:T(8,128)(2,1)} copy(bf16[1,128,1280]{2,1,0:T(8,128)(2,1)} %bitcast.10) | data formatting | bytes 655360

commit v4 on v3

--- a/solution.py
+++ b/solution.py
@@ -20,11 +20,16 @@
 NE = 32
 COL = 256
 NC = D // COL
-MSG = 48
+PW = 896
+FW = D - PW
+MSG = 32
+FMSG = 48
 HALF = 16
 CR = HALF * CAP
 GS = 8
 GM = GS * MSG
+FGM = GS * FMSG
+ALLF = NE * FMSG
 ALL = NE * MSG
 EPS = 1e-06
 NEG = -1e30
@@ -71,11 +76,14 @@
 
 def kernel(
     tok, seg, eid, gate, lna, lne, wqkv_h, wao_h, win_h, wout_h, out,
-    wqkv, wao, win, wout, xn, segs, q, k, v, ctx, ctxb, mid, xp, g, send, rcv, a, hid,
-    part, keep, own, stage, back, rst, pack, ret, pick, unp0, unp1, pkm0, pkm1, gcol,
+    wqkv, wao, win, wout, xn, info, q, k, v, ctx, ctxb, mid, xp, g, send, rcv, a, hid,
+    part, keep, own, stage, back, rst, pack, ret, unp0, unp1, pkm0, pkm1, gcol,
+    zx, gf, fsend, frcv, unf, pkf, frst, fpack, fret, fpart, fout, fown, fstage, fback,
     w_sem, as_sem, ar_sem, ss_sem, sr_sem, ds_sem, dr_sem, zs_sem, zr_sem, bs_sem, br_sem,
-    es_sem, er_sem,
+    es_sem, er_sem, xs_sem, xr_sem, fds_sem, fdr_sem, fes_sem, fer_sem, ys_sem, yr_sem,
 ):
+    pick = wqkv.at[:, pl.ds(0, ALL)]
+    fpick = wqkv.at[pl.ds(0, 4 * 256), pl.ds(ALL, ALLF)]
     d = lax.axis_index("dp")
     z = lax.axis_index("seq")
     zl = lax.rem(z + 3, 4)
@@ -91,8 +99,11 @@
         dx, dy, dc = OFFSETS[n]
         return xs[sign * dx % 4] + ys[sign * dy % 4] + cs[dc]
 
-    def rows48(j):
+    def rows_of(j):
         return pl.ds(pl.multiple_of(j * MSG, MSG), MSG)
+
+    def frows_of(j):
+        return pl.ds(pl.multiple_of(j * FMSG, FMSG), FMSG)
 
     loads = []
     for i in range(3):
@@ -111,7 +122,32 @@
     for n in range(NE - 1):
         pl.semaphore_signal(barrier, inc=1, device_id=(shifted(n, 1), z), device_id_type=MESH)
     xn[pl.ds(0, TOK), :] = normalize(tok[...].astype(F32), lna[...].reshape(1, D)).astype(BF16)
-    segs[0] = jnp.broadcast_to(seg[...], (8, TOK))
+
+    e0, e1 = eid[0:1, :], eid[1:2, :]
+    ei = iota((NE, TOK), 0)
+    named = jnp.where((ei == e0) | (ei == e1), 1.0, 0.0).astype(BF16)
+    before = jnp.where(iota((TOK, TOK), 0) < iota((TOK, TOK), 1), 1.0, 0.0).astype(BF16)
+    count = dot(named, before)
+    chosen = []
+    lines = [seg[...].astype(F32)]
+    for e in (e0, e1):
+        slot = jnp.sum(jnp.where(ei == e, count, 0.0), axis=0, keepdims=True).astype(I32)
+        lines.append((e * FMSG + slot).astype(F32))
+        odd = slot & 1
+        pair = e * MSG + 3 * CAP + lax.shift_right_logical(slot, 1)
+        chosen.append(
+            (e * MSG + slot, jnp.where(odd == 0, pair, -1), jnp.where(odd == 1, pair, -1))
+        )
+    lines += [gate[0:1, :], gate[1:2, :]]
+    ri = iota((8, TOK), 0)
+
+    def stacked_lines(rows):
+        total = jnp.zeros((8, TOK), F32)
+        for n, row in enumerate(rows):
+            total = jnp.where(ri == n, row, total)
+        return total
+
+    info[0] = stacked_lines(lines)
     pl.semaphore_wait(barrier, NE - 1 + 3)
 
     def remote(src, dst, s_sem, r_sem, dev):
@@ -126,9 +162,9 @@
         return xn.at[pl.ds(slot * TOK + half * 64, 64), :]
 
     seg_copies = [
-        remote(segs.at[0], segs.at[1], ss_sem.at[0], sr_sem.at[0], right),
-        remote(segs.at[0], segs.at[2], ss_sem.at[1], sr_sem.at[1], left),
-        remote(segs.at[0], segs.at[3], ss_sem.at[2], sr_sem.at[2], across),
+        remote(info.at[0], info.at[1], ss_sem.at[0], sr_sem.at[0], right),
+        remote(info.at[0], info.at[2], ss_sem.at[1], sr_sem.at[1], left),
+        remote(info.at[0], info.at[3], ss_sem.at[2], sr_sem.at[2], across),
     ]
     r0 = remote(xrows(0, 0), xrows(1, 0), as_sem.at[0], ar_sem.at[0], right)
     r1 = remote(xrows(0, 1), xrows(1, 1), as_sem.at[1], ar_sem.at[1], right)
@@ -145,44 +181,34 @@
     for load in loads[3:]:
         load.start()
 
-    e0, e1 = eid[0:1, :], eid[1:2, :]
-    ei = iota((NE, TOK), 0)
-    named = jnp.where((ei == e0) | (ei == e1), 1.0, 0.0).astype(BF16)
-    before = jnp.where(iota((TOK, TOK), 0) < iota((TOK, TOK), 1), 1.0, 0.0).astype(BF16)
-    count = dot(named, before)
-    s0 = jnp.sum(jnp.where(ei == e0, count, 0.0), axis=0, keepdims=True)
-    s1 = jnp.sum(jnp.where(ei == e1, count, 0.0), axis=0, keepdims=True)
-    t0 = e0.astype(F32) * MSG + s0
-    t1 = e1.astype(F32) * MSG + s1
-    ri = iota((TOK, TOK), 0)
-    square = jnp.where(
-        ri == 0, t0, jnp.where(ri == 1, t1, jnp.where(ri == 2, gate[0:1, :], gate[1:2, :]))
-    )
-    gcol[...] = jnp.transpose(square)
-    t0, t1 = t0.astype(I32), t1.astype(I32)
+    def place(kind, cc):
+        return chosen[kind][0] + CAP * cc if cc < 3 else chosen[kind][cc - 2]
 
     def make_g(i):
         rows = pl.ds(i * 256, 256)
         r = iota((256, TOK), 0) + i * 256
         for cc in range(NC):
-            hit = (r == t0 + CAP * cc) | (r == t1 + CAP * cc)
+            hit = (r == place(0, cc)) | (r == place(1, cc))
             g[rows, cc * TOK : (cc + 1) * TOK] = jnp.where(hit, 1.0, 0.0).astype(BF16)
 
     each(ALL // 256, make_g)
 
-    def fixed(ref, q_dim, rows, first, base):
+    def fixed(ref, q_dim, rows, first, base, msg):
         q = iota(ref.shape, q_dim)
         r = iota(ref.shape, 1 - q_dim) + base
-        if rows == 64:
-            cc = lax.shift_right_logical(q, 6)
-        else:
-            cc = lax.shift_right_logical(q * 205, 14)
+        times, shift = {64: (1, 6), 80: (205, 14), CR: (1821, 18)}[rows]
+        cc = lax.shift_right_logical(q * times, shift)
         i = q - cc * rows + first
-        at = i + (MSG - CAP) * lax.shift_right_logical(i * 57, 9) + CAP * cc
+        source = lax.shift_right_logical(i * 57, 9)
+        slot = i - CAP * source
+        at = source * msg + CAP * cc + slot
+        if msg == MSG:
+            pair = source * msg + 3 * CAP + lax.shift_right_logical(slot, 1)
+            at = jnp.where(cc < 3, at, jnp.where((slot & 1) == cc - 3, pair, -1))
         ref[...] = jnp.where(r == at, 1.0, 0.0).astype(BF16)
 
-    fixed(unp0, 0, 64, 0, 0)
-    fixed(unp1, 0, 80, 64, 7 * MSG)
+    fixed(unp0, 0, 64, 0, 0, MSG)
+    fixed(unp1, 0, 80, 64, 7 * MSG, MSG)
 
     r0.wait_recv()
     ro.start()
@@ -207,30 +233,32 @@
         each(NC, step)
 
     keys_values(0, TOK)
-    fixed(pkm0, 1, 80, 0, 0)
-    fixed(pkm1, 1, 80, 64, GM)
+    fixed(pkm0, 1, 80, 0, 0, MSG)
+    fixed(pkm1, 1, 80, 64, GM, MSG)
+    fixed(unf, 0, CR, 0, 0, FMSG)
+    fixed(pkf, 1, CR, 0, 0, FMSG)
 
     r1.wait_recv()
     l0.wait_recv()
     keys_values(TOK, 2 * TOK)
 
-    ri = iota((TOK, ALL), 1)
-    c0, c1 = gcol[:, 0:1].astype(I32), gcol[:, 1:2].astype(I32)
-
-    def make_pick(cc):
-        base = cc * 256
-        pick[pl.ds(base, TOK), :] = jnp.where(ri == c0 + CAP * cc, 1.0, 0.0).astype(BF16)
-        pick[pl.ds(base + TOK, TOK), :] = jnp.where(ri == c1 + CAP * cc, 1.0, 0.0).astype(BF16)
-
-    each(NC, make_pick)
-
     for copy in seg_copies:
         copy.wait_recv()
-    eight = iota((8, TOK), 0)
-    kinds = [jnp.where(eight == segs[s], 1.0, 0.0).astype(BF16) for s in range(4)]
+    eight = iota((8, TOK), 0).astype(F32)
+    kinds = [jnp.where(eight == info[s, 0:1, :], 1.0, 0.0).astype(BF16) for s in range(4)]
     key_kind = jnp.concatenate(kinds, axis=1)
     same = lax.dot_general(kinds[0], key_kind, (((0,), (0,)), ((), ())), preferred_element_type=F32)
     bias = jnp.where(same > 0.5, 0.0, NEG)
+
+    for s in range(4):
+        more = jnp.zeros((8, TOK), F32)
+        if s == 0:
+            more = stacked_lines([row.astype(F32) for kind in chosen for row in kind])
+        square = jnp.concatenate([info[s], more, jnp.zeros((TOK - 16, TOK), F32)], axis=0)
+        gcol[s] = jnp.transpose(square)
+        r = iota((ALLF, TOK), 0) - CAP * s
+        f0, f1 = info[s, 1:2, :].astype(I32), info[s, 2:3, :].astype(I32)
+        gf[:, s * TOK : (s + 1) * TOK] = jnp.where((r == f0) | (r == f1), 1.0, 0.0).astype(BF16)
 
     ro.wait_recv()
     lo.wait_recv()
@@ -269,8 +297,27 @@
 
     each(NC, project)
     expert_in = normalize(mid[...], lne[...].reshape(1, D)).astype(BF16)
-    for cc in range(NC):
+    zx[pl.ds(0, TOK), :] = expert_in[:, PW:]
+
+    def zrows(slot, half):
+        return zx.at[pl.ds(slot * TOK + half * 64, 64), :]
+
+    xr0 = remote(zrows(0, 0), zrows(1, 0), xs_sem.at[0], xr_sem.at[0], right)
+    xr1 = remote(zrows(0, 1), zrows(1, 1), xs_sem.at[1], xr_sem.at[1], right)
+    xl1 = remote(zrows(0, 1), zrows(2, 1), xs_sem.at[2], xr_sem.at[2], left)
+    xl0 = remote(zrows(0, 0), zrows(2, 0), xs_sem.at[3], xr_sem.at[3], left)
+    xro = remote(zrows(1, 0), zrows(3, 0), xs_sem.at[4], xr_sem.at[4], right)
+    xlo = remote(zrows(2, 1), zrows(3, 1), xs_sem.at[5], xr_sem.at[5], left)
+    ring = [xr0, xr1, xl1, xl0, xro, xlo]
+    for copy in ring[:4]:
+        copy.start()
+
+    for cc in range(3):
         xp[pl.ds(cc * TOK, TOK), :] = expert_in[:, cc * COL : (cc + 1) * COL]
+    rest = expert_in[:, 3 * COL : PW]
+    none = jnp.zeros_like(rest)
+    xp[pl.ds(3 * TOK, TOK), :] = jnp.concatenate([rest, none], axis=1)
+    xp[pl.ds(4 * TOK, TOK), :] = jnp.concatenate([none, rest], axis=1)
 
     def fill(i):
         rows = pl.ds(i * 256, 256)
@@ -281,13 +328,13 @@
     for n in range(NE - 1):
         dest = shifted(n, 1)
         remote(
-            send.at[rows48(dest), :], rcv.at[rows48(n), :], ds_sem, dr_sem.at[n // GS], (dest, z)
+            send.at[rows_of(dest), :], rcv.at[rows_of(n), :], ds_sem, dr_sem.at[n // GS], (dest, z)
         ).start()
-    rcv[pl.ds((NE - 1) * MSG, MSG), :] = send[rows48(d), :]
+    rcv[pl.ds((NE - 1) * MSG, MSG), :] = send[rows_of(d), :]
 
     def piece_of(slot, half, n):
         first, number = OUT[n]
-        return a.at[slot, half, pl.ds(first, number)]
+        return a.at[slot, half, pl.ds(first, number), pl.ds(0, PW)]
 
     def arrived(group):
         number = GS if group < 3 else GS - 1
@@ -302,10 +349,14 @@
             got = dot(unp0[...], rcv[pl.ds(base, GM), :])
         else:
             got = dot(unp1[...], rcv[pl.ds(base + 7 * MSG, 9 * MSG), :])
-        for cc in range(NC):
-            a[0, half, first : first + number, cc * COL : (cc + 1) * COL] = got[
+        rows = slice(first, first + number)
+        for cc in range(3):
+            a[0, half, rows, cc * COL : (cc + 1) * COL] = got[
                 cc * number : (cc + 1) * number
             ].astype(BF16)
+        a[0, half, rows, 3 * COL : PW] = (
+            got[3 * number : 4 * number, :128] + got[4 * number :, 128:]
+        ).astype(BF16)
 
     zc = {}
     for half in range(2):
@@ -330,11 +381,11 @@
             hid[:, cols(j)] = gelu(dot(a[slot, half], win[:, cols(j)])).astype(BF16)
 
         each(NC, first)
-
-        def second(j):
+        for j in range(3):
             store(cols(j), dot(hid[...], wout[:, cols(j)]))
-
-        each(NC, second)
+        value = dot(hid[...], wout[:, 3 * COL :])
+        store(pl.ds(3 * COL, 128), value[:, :128])
+        frst[half, pl.ds(slot * CR, CR), :] = value[:, 128:].astype(BF16)
 
     def into_own(half):
         def store(at, value):
@@ -378,38 +429,92 @@
     loads[4].wait()
     loads[5].wait()
 
-    for half in range(2):
-        for n in range(2):
-            unpack(half, n)
-            zc["r", half, n].start()
-            zc["l", half, n].start()
+    xr0.wait_recv()
+    xro.start()
+    xl1.wait_recv()
+    xlo.start()
+    for n in range(2):
+        unpack(0, n)
+        zc["r", 0, n].start()
+        zc["l", 0, n].start()
+    for copy in (xr1, xl0, xro, xlo):
+        copy.wait_recv()
+    for i in range(ALLF // 256):
+        rows = pl.ds(i * 256, 256)
+        fsend[rows, :] = dot(gf[rows, :], zx[...]).astype(BF16)
+    for n in range(NE - 1):
+        dest = shifted(n, 1)
+        remote(
+            fsend.at[frows_of(dest), :], frcv.at[frows_of(n), :],
+            fds_sem, fdr_sem.at[n // HALF], (dest, z),
+        ).start()
+    frcv[pl.ds((NE - 1) * FMSG, FMSG), :] = fsend[frows_of(d), :]
+    for n in range(2):
+        unpack(1, n)
+        zc["r", 1, n].start()
+        zc["l", 1, n].start()
+
+    ri = iota((TOK, ALL), 1)
+    for cc in range(NC):
+        line = 8 if cc < 3 else 6 + cc
+        for kind in range(2):
+            at = gcol[0, :, line + 3 * kind : line + 3 * kind + 1].astype(I32)
+            at = at + CAP * cc if cc < 3 else at
+            pick[pl.ds(cc * 256 + kind * TOK, TOK), :] = jnp.where(ri == at, 1.0, 0.0).astype(BF16)
     for n in range(2):
         zc["r", 0, n].wait_recv()
         zc["ro", n].start()
-    expert(0, 0, into_own(0))
+    fi = iota((TOK, ALLF), 1)
+    for s in range(4):
+        for kind in range(2):
+            at = gcol[s, :, 1 + kind : 2 + kind].astype(I32) + CAP * s
+            fpick[pl.ds(s * 256 + kind * TOK, TOK), :] = jnp.where(fi == at, 1.0, 0.0).astype(BF16)
     for n in range(2):
         zc["l", 1, n].wait_recv()
         zc["lo", n].start()
+
+    def funpack(half):
+        number = HALF if half == 0 else HALF - 1
+        got = frcv.at[pl.ds(half * HALF * FMSG, number * FMSG), :]
+        remote(got, got, fds_sem, fdr_sem.at[half], right).wait_recv()
+        rows = dot(unf[...], frcv[pl.ds(half * HALF * FMSG, HALF * FMSG), :]).astype(BF16)
+        for s in range(4):
+            a[s, half, :, PW:] = rows[s * CR : (s + 1) * CR]
+
+    def freturn(half):
+        fpack[pl.ds(half * HALF * FMSG, HALF * FMSG), :] = dot(pkf[...], frst[half]).astype(BF16)
+        for m in range(half * HALF, min((half + 1) * HALF, NE - 1)):
+            dest = shifted(m, -1)
+            remote(
+                fpack.at[frows_of(m), :], fret.at[frows_of(d), :], fes_sem, fer_sem, (dest, z)
+            ).start()
+
+    funpack(0)
     expert(1, 0, into_part(0))
     b_left0.start()
-    expert(2, 1, into_part(1))
-    b_right1.start()
-    for n in range(2):
-        zc["r", 1, n].wait_recv()
+    for n in range(2):
         zc["l", 0, n].wait_recv()
     expert(2, 0, into_keep(0))
-    expert(1, 1, into_keep(1))
-    expert(0, 1, into_own(1))
+    expert(0, 0, into_own(0))
     for n in range(2):
         zc["ro", n].wait_recv()
     expert(3, 0, into_part(2))
     bc["across0", 0].start()
     bc["across0", 1].start()
-    for n in range(2):
+    freturn(0)
+    for n in range(2):
+        zc["r", 1, n].wait_recv()
         zc["lo", n].wait_recv()
+    funpack(1)
     expert(3, 1, into_part(3))
     bc["across1", 0].start()
     bc["across1", 1].start()
+    expert(2, 1, into_part(1))
+    b_right1.start()
+    expert(1, 1, into_keep(1))
+    expert(0, 1, into_own(1))
+    freturn(1)
+    fret[frows_of(d), :] = fpack[pl.ds((NE - 1) * FMSG, FMSG), :]
     for n in range(2):
         first, number = BACK[n]
         rows = pl.ds(first, number)
@@ -420,46 +525,102 @@
         part[5, rows] = (keep[1, rows] + stage[1, rows].astype(F32)).astype(BF16)
         bc["left1", n].start()
 
+    def half_of(ref, slot, n):
+        return ref.at[slot, pl.ds(n * 64, 64)]
+
+    ya0 = remote(half_of(fout, 3, 0), fstage.at[0], ys_sem.at[0], yr_sem.at[0], right)
+    ya1 = remote(half_of(fout, 3, 1), fstage.at[1], ys_sem.at[1], yr_sem.at[1], left)
+    yl0 = remote(half_of(fout, 1, 0), half_of(fback, 1, 0), ys_sem.at[2], yr_sem.at[2], left)
+    yr1 = remote(half_of(fout, 2, 1), half_of(fback, 0, 1), ys_sem.at[3], yr_sem.at[3], right)
+    yr0 = remote(half_of(fout, 2, 0), half_of(fback, 0, 0), ys_sem.at[4], yr_sem.at[4], right)
+    yl1 = remote(half_of(fout, 1, 1), half_of(fback, 1, 1), ys_sem.at[5], yr_sem.at[5], left)
+    ring += [ya0, ya1, yl0, yr1, yr0, yl1]
+
     b_left0.wait_recv()
     b_right1.wait_recv()
-    for n in range(2):
+    def finish(n):
         first, number = BACK[n]
         rows = pl.ds(first, number)
         for half in range(2):
             bc["right0" if half == 0 else "left1", n].wait_recv()
-            for cc in range(NC):
-                at = slice(cc * COL, (cc + 1) * COL)
+            for cc in range(4):
+                at = slice(cc * COL, min((cc + 1) * COL, PW))
                 full = (
                     own[half, rows, at]
                     + back[half, rows, at].astype(F32)
                     + back[2 + half, rows, at].astype(F32)
                 ).astype(BF16)
-                if n == 0:
-                    rst[half, 0, pl.ds(cc * 80, 80), :] = full
-                    rst[half, 1, pl.ds(cc * 80, 16), :] = full[64:]
-                else:
-                    rst[half, 1, pl.ds(cc * 80 + 16, 64), :] = full
+                both = [full]
+                if cc == 3:
+                    none = jnp.zeros_like(full)
+                    both = [
+                        jnp.concatenate([full, none], axis=1),
+                        jnp.concatenate([none, full], axis=1),
+                    ]
+                for m, value in enumerate(both):
+                    if n == 0:
+                        rst[half, 0, pl.ds((cc + m) * 80, 80), :] = value
+                        rst[half, 1, pl.ds((cc + m) * 80, 16), :] = value[64:]
+                    else:
+                        rst[half, 1, pl.ds((cc + m) * 80 + 16, 64), :] = value
             packed = dot((pkm0 if n == 0 else pkm1)[...], rst[half, n])
             group = 2 * half + n
             pack[pl.ds(group * GM, GM), :] = packed.astype(BF16)
             for m in range(group * GS, min((group + 1) * GS, NE - 1)):
                 dest = shifted(m, -1)
                 remote(
-                    pack.at[rows48(m), :], ret.at[rows48(d), :], es_sem, er_sem, (dest, z)
+                    pack.at[rows_of(m), :], ret.at[rows_of(d), :], es_sem, er_sem, (dest, z)
                 ).start()
-    ret[rows48(d), :] = pack[pl.ds((NE - 1) * MSG, MSG), :]
+    finish(0)
+
+    others = fret.at[pl.ds(0, (NE - 1) * FMSG), :]
+    remote(others, others, fes_sem, fer_sem, right).wait_recv()
+    for s in (3, 1, 2, 0):
+        both = dot(fpick[pl.ds(s * 256, 256), :], fret[...])
+        sums = gcol[s, :, 3:4] * both[:TOK] + gcol[s, :, 4:5] * both[TOK:]
+        if s == 0:
+            fown[...] = sums
+        else:
+            fpart[s] = sums
+            for n in range(2):
+                rows = pl.ds(n * 64, 64)
+                fout[s, rows] = sums[n * 64 : (n + 1) * 64].astype(BF16)
+        if s == 3:
+            ya0.start()
+            ya1.start()
+        if s == 1:
+            yl0.start()
+        if s == 2:
+            yr1.start()
+
+    finish(1)
+    ret[rows_of(d), :] = pack[pl.ds((NE - 1) * MSG, MSG), :]
+
+    ya0.wait_recv()
+    fout[2, pl.ds(0, 64)] = (fpart[2, pl.ds(0, 64)] + fstage[0].astype(F32)).astype(BF16)
+    yr0.start()
+    ya1.wait_recv()
+    fout[1, pl.ds(64, 64)] = (fpart[1, pl.ds(64, 64)] + fstage[1].astype(F32)).astype(BF16)
+    yl1.start()
 
     others = ret.at[pl.ds(0, (NE - 1) * MSG), :]
     remote(others, others, es_sem, er_sem, right).wait_recv()
-    g0, g1 = gcol[:, 2:3], gcol[:, 3:4]
-
-    def final(cc):
+    g0, g1 = gcol[0, :, 3:4], gcol[0, :, 4:5]
+    for cc in range(3):
         both = dot(pick[pl.ds(cc * 256, 256), :], ret[...])
         out[:, cols(cc)] = (mid[:, cols(cc)] + g0 * both[:TOK] + g1 * both[TOK:]).astype(BF16)
-
-    each(NC, final)
-
-    for copy in seg_copies + [r0, r1, l0, l1, ro, lo] + list(zc.values()):
+    even = dot(pick[pl.ds(3 * 256, 256), :], ret[...])[:, :128]
+    both = even + dot(pick[pl.ds(4 * 256, 256), :], ret[...])[:, 128:]
+    out[:, 3 * COL : PW] = (
+        mid[:, 3 * COL : PW] + g0 * both[:TOK] + g1 * both[TOK:]
+    ).astype(BF16)
+    for copy in (yl0, yr1, yr0, yl1):
+        copy.wait_recv()
+    out[:, PW:] = (
+        mid[:, PW:] + fown[...] + fback[0].astype(F32) + fback[1].astype(F32)
+    ).astype(BF16)
+
+    for copy in seg_copies + [r0, r1, l0, l1, ro, lo] + ring + list(zc.values()):
         copy.wait_send()
     for copy in [b_left0, b_right1] + list(bc.values()):
         copy.wait_send()
@@ -467,6 +628,10 @@
     remote(gone, gone, ds_sem, dr_sem.at[0], right).wait_send()
     gone = pack.at[pl.ds(0, (NE - 1) * MSG), :]
     remote(gone, gone, es_sem, er_sem, right).wait_send()
+    gone = fsend.at[pl.ds(0, (NE - 1) * FMSG), :]
+    remote(gone, gone, fds_sem, fdr_sem.at[0], right).wait_send()
+    gone = fpack.at[pl.ds(0, (NE - 1) * FMSG), :]
+    remote(gone, gone, fes_sem, fer_sem, right).wait_send()
 
 
 def layer(tok, seg, eid, gate, lna, lne, wqkv, wao, win, wout):
@@ -485,7 +650,7 @@
             V((D, D), BF16),
             V((D, D), BF16),
             V((4 * TOK, D), BF16),
-            V((4, 8, TOK), I32),
+            V((4, 8, TOK), F32),
             V((TOK, D), BF16),
             V((4 * TOK, D), BF16),
             V((4 * TOK, D), BF16),
@@ -498,20 +663,33 @@
             V((ALL, COL), BF16),
             V((4, 2, CR, D), BF16),
             V((CR, D), BF16),
-            V((6, CR, D), BF16),
-            V((2, CR, D), F32),
-            V((2, CR, D), F32),
-            V((2, CR, D), BF16),
-            V((4, CR, D), BF16),
+            V((6, CR, PW), BF16),
+            V((2, CR, PW), F32),
+            V((2, CR, PW), F32),
+            V((2, CR, PW), BF16),
+            V((4, CR, PW), BF16),
             V((2, 2, NC * 80, COL), BF16),
             V((ALL, COL), BF16),
             V((ALL, COL), BF16),
-            V((2 * NC * TOK, ALL), BF16),
             V((NC * 64, GM), BF16),
             V((NC * 80, 9 * MSG), BF16),
             V((GM, NC * 80), BF16),
             V((GM, NC * 80), BF16),
-            V((TOK, TOK), F32),
+            V((4, TOK, TOK), F32),
+            V((4 * TOK, FW), BF16),
+            V((ALLF, 4 * TOK), BF16),
+            V((ALLF, FW), BF16),
+            V((ALLF, FW), BF16),
+            V((4 * CR, HALF * FMSG), BF16),
+            V((HALF * FMSG, 4 * CR), BF16),
+            V((2, 4 * CR, FW), BF16),
+            V((ALLF, FW), BF16),
+            V((ALLF, FW), BF16),
+            V((4, TOK, FW), F32),
+            V((4, TOK, FW), BF16),
+            V((TOK, FW), F32),
+            V((2, 64, FW), BF16),
+            V((2, TOK, FW), BF16),
             dma((6,)),
             dma((6,)),
             dma((6,)),
@@ -525,6 +703,14 @@
             dma((10,)),
             dma,
             dma,
+            dma((6,)),
+            dma((6,)),
+            dma,
+            dma((2,)),
+            dma,
+            dma,
+            dma((6,)),
+            dma((6,)),
         ],
         compiler_params=pltpu.CompilerParams(
             collective_id=0, has_side_effects=True, vmem_limit_bytes=60 * 1024 * 1024

time: 96.8 us -> 83.8 us (0.87)
  Pallas kernels: 94.9 us -> 81.9 us
    pallas_call x1, Pallas kernels: 94.9 us -> 81.9 us  [layer(): pl.pallas_call(kernel, out_shape=jax.ShapeDtypeStruct((TOK, D), BF16), in...]
where the time goes in v4:
time: 83.8 us; the launch traced here: 83.6 us
  Pallas kernels  81.9 us (98%)
  local copies, waits for them, and re-layouts  1.72 us (2%)
    pallas_call x1, Pallas kernels, layer(): pl.pallas_call(kernel, out_shape=jax.ShapeDtypeStruct((TOK, D), BF16), in...  81.9 us
    unnamed x1, local copies, waits for them, and re-layouts  1.72 us

profile of v4, /device:TPU:1, one launch (start us, length us, event | category | flops | bytes accessed | tf_op | source)
XLA Modules:
  0.0 83.6 jit_solution(16984133819169300012)
XLA Ops:
  0.0 81.9 %shard_map.100 = bf16[128,1280]{1,0:T(8,128)(2,1)} custom-call(bf16[128,1280]{1,0:T(8,128)(2,1)} %bitcast.13, s32[1,128]{1,0:T(1,128)} %seg.1, s32[2,128]{1,0:T(2,128)} %bitcast.14, f32[2,128]{1,0:T(2,128)} %bitcast.15, f32[1280]{0:T(1024)} %lna.1, f32[1280]{0:T(1024)} %lne.1, bf16[1280,3840]{1,0:T(8,128)(2,1)} %wqkv_h.1, bf16[1280,1280]{1,0:T(8,128)(2,1)} %wao_h.1, ...), custom_call_target="tpu_custom_call" | custom-call | flops 14000000000 | bytes 24000000 | tf_op jit(solution)/shard_map/pallas_call | solution.py:642
  81.9 1.7 %copy.12 = bf16[1,128,1280]{2,1,0:T(8,128)(2,1)} copy(bf16[1,128,1280]{2,1,0:T(8,128)(2,1)} %bitcast.10) | data formatting | bytes 655360

commit v5 on v4

--- a/solution.py
+++ b/solution.py
@@ -80,7 +80,7 @@
     part, keep, own, stage, back, rst, pack, ret, unp0, unp1, pkm0, pkm1, gcol,
     zx, gf, fsend, frcv, unf, pkf, frst, fpack, fret, fpart, fout, fown, fstage, fback,
     w_sem, as_sem, ar_sem, ss_sem, sr_sem, ds_sem, dr_sem, zs_sem, zr_sem, bs_sem, br_sem,
-    es_sem, er_sem, xs_sem, xr_sem, fds_sem, fdr_sem, fes_sem, fer_sem, ys_sem, yr_sem,
+    es_sem, er_sem, round_sem, xs_sem, xr_sem, fds_sem, fdr_sem, fes_sem, fer_sem, ys_sem, yr_sem,
 ):
     pick = wqkv.at[:, pl.ds(0, ALL)]
     fpick = wqkv.at[pl.ds(0, 4 * 256), pl.ds(ALL, ALLF)]
@@ -119,8 +119,11 @@
     for other in (zl, zr, zo):
         pl.semaphore_signal(barrier, inc=1, device_id=(d, other), device_id_type=MESH)
 
-    for n in range(NE - 1):
-        pl.semaphore_signal(barrier, inc=1, device_id=(shifted(n, 1), z), device_id_type=MESH)
+    x_line = [xs[i] + ys[0] + cs[0] for i in range(1, 4)]
+    y_line = [xs[0] + ys[i] + cs[0] for i in range(1, 4)]
+    twin = xs[0] + ys[0] + cs[1]
+    for other in x_line + y_line + [twin]:
+        pl.semaphore_signal(barrier, inc=1, device_id=(other, z), device_id_type=MESH)
     xn[pl.ds(0, TOK), :] = normalize(tok[...].astype(F32), lna[...].reshape(1, D)).astype(BF16)
 
     e0, e1 = eid[0:1, :], eid[1:2, :]
@@ -148,7 +151,7 @@
         return total
 
     info[0] = stacked_lines(lines)
-    pl.semaphore_wait(barrier, NE - 1 + 3)
+    pl.semaphore_wait(barrier, 10)
 
     def remote(src, dst, s_sem, r_sem, dev):
         return pltpu.make_async_remote_copy(
@@ -180,6 +183,8 @@
         copy.start()
     for load in loads[3:]:
         load.start()
+    for other in x_line:
+        pl.semaphore_signal(round_sem.at[0], inc=1, device_id=(other, z), device_id_type=MESH)
 
     def place(kind, cc):
         return chosen[kind][0] + CAP * cc if cc < 3 else chosen[kind][cc - 2]
@@ -214,6 +219,9 @@
     ro.start()
     l1.wait_recv()
     lo.start()
+
+    pl.semaphore_wait(round_sem.at[0], 3)
+    pl.semaphore_signal(round_sem.at[1], inc=1, device_id=(twin, z), device_id_type=MESH)
 
     for load in loads[:3]:
         load.wait()
@@ -325,6 +333,7 @@
 
     each(ALL // 256, fill)
 
+    pl.semaphore_wait(round_sem.at[1], 1)
     for n in range(NE - 1):
         dest = shifted(n, 1)
         remote(
@@ -703,6 +712,7 @@
             dma((10,)),
             dma,
             dma,
+            pltpu.SemaphoreType.REGULAR((2,)),
             dma((6,)),
             dma((6,)),
             dma,
@@ -713,7 +723,7 @@
             dma((6,)),
         ],
         compiler_params=pltpu.CompilerParams(
-            collective_id=0, has_side_effects=True, vmem_limit_bytes=60 * 1024 * 1024
+            collective_id=0, has_side_effects=True, vmem_limit_bytes=50 * 1024 * 1024
         ),
         cost_estimate=pl.CostEstimate(
             flops=14_000_000_000, bytes_accessed=24_000_000, transcendentals=3_000_000

time: 83.8 us -> 86.3 us (1.030)
  local copies, waits for them, and re-layouts: 1.72 us -> 7.03 us
  Pallas kernels: 81.9 us -> 79 us
    unnamed x1 -> x15, local copies, waits for them, and re-layouts: 1.72 us -> 7.03 us
    pallas_call x1, Pallas kernels: 81.9 us -> 79 us  [layer(): pl.pallas_call(kernel, out_shape=jax.ShapeDtypeStruct((TOK, D), BF16), in...]
where the time goes in v5:
time: 86.3 us; the launch traced here: 86 us
  Pallas kernels  79 us (92%)
  local copies, waits for them, and re-layouts  7.03 us (8%)
    pallas_call x1, Pallas kernels, layer(): pl.pallas_call(kernel, out_shape=jax.ShapeDtypeStruct((TOK, D), BF16), in...  79 us
    unnamed x15, local copies, waits for them, and re-layouts  7.03 us

profile of v5, /device:TPU:1, one launch (start us, length us, event | category | flops | bytes accessed | tf_op | source)
XLA Modules:
  0.0 86.0 jit_solution(3698065389067791986)
XLA Ops:
  0.0 0.0 copy-start
  0.0 1.9 %copy-done = bf16[1280,1280]{1,0:T(8,128)(2,1)S(1)} copy-done((bf16[1280,1280]{1,0:T(8,128)(2,1)S(1)}, bf16[1280,1280]{1,0:T(8,128)(2,1)}, u32[]{:S(2)}) %copy-start) | copy-done | bytes 3276824
  1.9 0.0 copy-start.1
  1.9 1.0 %copy-done.1 = bf16[1,128,1280]{2,1,0:T(8,128)(2,1)S(1)} copy-done((bf16[1,128,1280]{2,1,0:T(8,128)(2,1)S(1)}, bf16[1,128,1280]{2,1,0:T(8,128)(2,1)}, u32[]{:S(2)}) %copy-start.1) | copy-done | bytes 327704
  2.9 0.0 copy-start.2
  2.9 0.7 copy-done.2
  3.6 0.0 copy-start.3
  3.6 0.7 copy-done.3
  4.3 0.0 copy-start.4
  4.3 0.7 copy-done.4
  5.0 0.0 copy-start.5
  5.0 0.7 copy-done.5
  5.7 0.0 copy-start.6
  5.7 0.7 copy-done.6
  6.3 79.0 %shard_map.100 = bf16[128,1280]{1,0:T(8,128)(2,1)S(1)} custom-call(bf16[128,1280]{1,0:T(8,128)(2,1)S(1)} %bitcast.11, s32[1,128]{1,0:T(1,128)S(1)} %copy-done.6, s32[2,128]{1,0:T(2,128)S(1)} %bitcast.12, f32[2,128]{1,0:T(2,128)S(1)} %bitcast.13, f32[1280]{0:T(1024)S(1)} %copy-done.2, f32[1280]{0:T(1024)S(1)} %copy-done.3, bf16[1280,3840]{1,0:T(8,128)(2,1)} %wqkv_h.1, ...), custom_call_target="tpu_custom_call" | custom-call | flops 14000000000 | bytes 24000000 | tf_op jit(solution)/shard_map/pallas_call | solution.py:651
  85.3 0.7 copy.12
Async XLA Ops:
  0.0 1.9 %copy-start = (bf16[1280,1280]{1,0:T(8,128)(2,1)S(1)}, bf16[1280,1280]{1,0:T(8,128)(2,1)}, u32[]{:S(2)}) copy-start(bf16[1280,1280]{1,0:T(8,128)(2,1)} %wao_h.1) | copy-start | bytes 9830404
  1.9 1.0 %copy-start.1 = (bf16[1,128,1280]{2,1,0:T(8,128)(2,1)S(1)}, bf16[1,128,1280]{2,1,0:T(8,128)(2,1)}, u32[]{:S(2)}) copy-start(bf16[1,128,1280]{2,1,0:T(8,128)(2,1)} %param.10) | copy-start | bytes 983044
  2.9 0.7 copy-start.2
  3.6 0.7 copy-start.3
  4.3 0.7 copy-start.4
  5.0 0.7 copy-start.5
  5.7 0.7 copy-start.6

commit v6 on v5

--- a/solution.py
+++ b/solution.py
@@ -75,11 +75,11 @@
 
 
 def kernel(
-    tok, seg, eid, gate, lna, lne, wqkv_h, wao_h, win_h, wout_h, out,
-    wqkv, wao, win, wout, xn, info, q, k, v, ctx, ctxb, mid, xp, g, send, rcv, a, hid,
+    tok_h, seg_h, eid_h, gate_h, lna_h, lne_h, wqkv_h, wao_h, win_h, wout_h, out,
+    tok, seg, eid, gate, lna, lne, wqkv, wao, win, wout, xn, xraw, info, q, k, v, ctx, ctxb, mid, xp, g, send, rcv, a, hid,
     part, keep, own, stage, back, rst, pack, ret, unp0, unp1, pkm0, pkm1, gcol,
     zx, gf, fsend, frcv, unf, pkf, frst, fpack, fret, fpart, fout, fown, fstage, fback,
-    w_sem, as_sem, ar_sem, ss_sem, sr_sem, ds_sem, dr_sem, zs_sem, zr_sem, bs_sem, br_sem,
+    i_sem, w_sem, as_sem, ar_sem, ss_sem, sr_sem, ds_sem, dr_sem, zs_sem, zr_sem, bs_sem, br_sem,
     es_sem, er_sem, round_sem, xs_sem, xr_sem, fds_sem, fdr_sem, fes_sem, fer_sem, ys_sem, yr_sem,
 ):
     pick = wqkv.at[:, pl.ds(0, ALL)]
@@ -105,6 +105,10 @@
     def frows_of(j):
         return pl.ds(pl.multiple_of(j * FMSG, FMSG), FMSG)
 
+    small = [(tok_h, tok), (lna_h, lna), (eid_h, eid), (seg_h, seg), (gate_h, gate), (lne_h, lne)]
+    small = [pltpu.make_async_copy(src, dst, i_sem.at[n]) for n, (src, dst) in enumerate(small)]
+    for copy in small:
+        copy.start()
     loads = []
     for i in range(3):
         part_of = pl.ds(i * D, D)
@@ -112,9 +116,6 @@
     loads.append(pltpu.make_async_copy(wao_h, wao, w_sem.at[3]))
     loads.append(pltpu.make_async_copy(win_h, win, w_sem.at[4]))
     loads.append(pltpu.make_async_copy(wout_h, wout, w_sem.at[5]))
-    for load in loads[:3]:
-        load.start()
-
     barrier = pltpu.get_barrier_semaphore()
     for other in (zl, zr, zo):
         pl.semaphore_signal(barrier, inc=1, device_id=(d, other), device_id_type=MESH)
@@ -124,7 +125,40 @@
     twin = xs[0] + ys[0] + cs[1]
     for other in x_line + y_line + [twin]:
         pl.semaphore_signal(barrier, inc=1, device_id=(other, z), device_id_type=MESH)
-    xn[pl.ds(0, TOK), :] = normalize(tok[...].astype(F32), lna[...].reshape(1, D)).astype(BF16)
+
+    pl.semaphore_wait(barrier, 10)
+
+    def remote(src, dst, s_sem, r_sem, dev):
+        return pltpu.make_async_remote_copy(
+            src_ref=src, dst_ref=dst, send_sem=s_sem, recv_sem=r_sem,
+            device_id=dev, device_id_type=MESH,
+        )
+
+    right, left, across = (d, zr), (d, zl), (d, zo)
+
+    def xrows(slot, half):
+        rows = pl.ds(slot * TOK + half * 64, 64)
+        return tok_h.at[pl.ds(half * 64, 64), :] if slot == 0 else xraw.at[rows, :]
+
+    seg_copies = [
+        remote(info.at[0], info.at[1], ss_sem.at[0], sr_sem.at[0], right),
+        remote(info.at[0], info.at[2], ss_sem.at[1], sr_sem.at[1], left),
+        remote(info.at[0], info.at[3], ss_sem.at[2], sr_sem.at[2], across),
+    ]
+    r0 = remote(xrows(0, 0), xrows(1, 0), as_sem.at[0], ar_sem.at[0], right)
+    r1 = remote(xrows(0, 1), xrows(1, 1), as_sem.at[1], ar_sem.at[1], right)
+    l1 = remote(xrows(0, 1), xrows(2, 1), as_sem.at[2], ar_sem.at[2], left)
+    l0 = remote(xrows(0, 0), xrows(2, 0), as_sem.at[3], ar_sem.at[3], left)
+    ro = remote(xrows(1, 0), xrows(3, 0), as_sem.at[4], ar_sem.at[4], right)
+    lo = remote(xrows(2, 1), xrows(3, 1), as_sem.at[5], ar_sem.at[5], left)
+    r0.start()
+    l1.start()
+    r1.start()
+    l0.start()
+    for load in loads:
+        load.start()
+    for copy in small:
+        copy.wait()
 
     e0, e1 = eid[0:1, :], eid[1:2, :]
     ei = iota((NE, TOK), 0)
@@ -151,38 +185,10 @@
         return total
 
     info[0] = stacked_lines(lines)
-    pl.semaphore_wait(barrier, 10)
-
-    def remote(src, dst, s_sem, r_sem, dev):
-        return pltpu.make_async_remote_copy(
-            src_ref=src, dst_ref=dst, send_sem=s_sem, recv_sem=r_sem,
-            device_id=dev, device_id_type=MESH,
-        )
-
-    right, left, across = (d, zr), (d, zl), (d, zo)
-
-    def xrows(slot, half):
-        return xn.at[pl.ds(slot * TOK + half * 64, 64), :]
-
-    seg_copies = [
-        remote(info.at[0], info.at[1], ss_sem.at[0], sr_sem.at[0], right),
-        remote(info.at[0], info.at[2], ss_sem.at[1], sr_sem.at[1], left),
-        remote(info.at[0], info.at[3], ss_sem.at[2], sr_sem.at[2], across),
-    ]
-    r0 = remote(xrows(0, 0), xrows(1, 0), as_sem.at[0], ar_sem.at[0], right)
-    r1 = remote(xrows(0, 1), xrows(1, 1), as_sem.at[1], ar_sem.at[1], right)
-    l1 = remote(xrows(0, 1), xrows(2, 1), as_sem.at[2], ar_sem.at[2], left)
-    l0 = remote(xrows(0, 0), xrows(2, 0), as_sem.at[3], ar_sem.at[3], left)
-    ro = remote(xrows(1, 0), xrows(3, 0), as_sem.at[4], ar_sem.at[4], right)
-    lo = remote(xrows(2, 1), xrows(3, 1), as_sem.at[5], ar_sem.at[5], left)
-    r0.start()
-    l1.start()
-    r1.start()
-    l0.start()
     for copy in seg_copies:
         copy.start()
-    for load in loads[3:]:
-        load.start()
+    xn[pl.ds(0, TOK), :] = normalize(tok[...].astype(F32), lna[...].reshape(1, D)).astype(BF16)
+
     for other in x_line:
         pl.semaphore_signal(round_sem.at[0], inc=1, device_id=(other, z), device_id_type=MESH)
 
@@ -233,6 +239,8 @@
 
     def keys_values(first, number):
         rows = pl.ds(first, number)
+        if first:
+            xn[rows, :] = normalize(xraw[rows, :].astype(F32), lna[...].reshape(1, D)).astype(BF16)
 
         def step(j):
             k[rows, cols(j)] = dot(xn[rows, :], wqkv[:, cols(j + NC)]).astype(BF16)
@@ -334,11 +342,21 @@
     each(ALL // 256, fill)
 
     pl.semaphore_wait(round_sem.at[1], 1)
-    for n in range(NE - 1):
-        dest = shifted(n, 1)
-        remote(
-            send.at[rows_of(dest), :], rcv.at[rows_of(n), :], ds_sem, dr_sem.at[n // GS], (dest, z)
-        ).start()
+
+    def to_experts(first, last):
+        for n in range(first, last):
+            dest = shifted(n, 1)
+            remote(
+                send.at[rows_of(dest), :], rcv.at[rows_of(n), :],
+                ds_sem, dr_sem.at[n // GS], (dest, z),
+            ).start()
+
+    to_experts(0, HALF)
+    xr0.wait_recv()
+    xro.start()
+    xl1.wait_recv()
+    xlo.start()
+    to_experts(HALF, NE - 1)
     rcv[pl.ds((NE - 1) * MSG, MSG), :] = send[rows_of(d), :]
 
     def piece_of(slot, half, n):
@@ -438,10 +456,6 @@
     loads[4].wait()
     loads[5].wait()
 
-    xr0.wait_recv()
-    xro.start()
-    xl1.wait_recv()
-    xlo.start()
     for n in range(2):
         unpack(0, n)
         zc["r", 0, n].start()
@@ -651,13 +665,20 @@
     return pl.pallas_call(
         kernel,
         out_shape=jax.ShapeDtypeStruct((TOK, D), BF16),
-        in_specs=[vm] * 6 + [hbm] * 4,
+        in_specs=[hbm] * 10,
         out_specs=vm,
         scratch_shapes=[
+            V((TOK, D), BF16),
+            V((1, TOK), I32),
+            V((2, TOK), I32),
+            V((2, TOK), F32),
+            V((D,), F32),
+            V((D,), F32),
             V((D, 3 * D), BF16),
             V((D, D), BF16),
             V((D, D), BF16),
             V((D, D), BF16),
+            V((4 * TOK, D), BF16),
             V((4 * TOK, D), BF16),
             V((4, 8, TOK), F32),
             V((TOK, D), BF16),
@@ -702,6 +723,7 @@
             dma((6,)),
             dma((6,)),
             dma((6,)),
+            dma((6,)),
             dma((3,)),
             dma((3,)),
             dma,
@@ -723,7 +745,7 @@
             dma((6,)),
         ],
         compiler_params=pltpu.CompilerParams(
-            collective_id=0, has_side_effects=True, vmem_limit_bytes=50 * 1024 * 1024
+            collective_id=0, has_side_effects=True, vmem_limit_bytes=60 * 1024 * 1024
         ),
         cost_estimate=pl.CostEstimate(
             flops=14_000_000_000, bytes_accessed=24_000_000, transcendentals=3_000_000

time: 86.3 us -> 82.3 us (0.954)
  local copies, waits for them, and re-layouts: 7.03 us -> 1.72 us
  Pallas kernels: 79 us -> 80.4 us
    unnamed x15 -> x1, local copies, waits for them, and re-layouts: 7.03 us -> 1.72 us
    pallas_call x1, Pallas kernels: 79 us -> 80.4 us  [layer(): pl.pallas_call(kernel, out_shape=jax.ShapeDtypeStruct((TOK, D), BF16), in...]
where the time goes in v6:
time: 82.3 us; the launch traced here: 82.2 us
  Pallas kernels  80.4 us (98%)
  local copies, waits for them, and re-layouts  1.72 us (2%)
    pallas_call x1, Pallas kernels, layer(): pl.pallas_call(kernel, out_shape=jax.ShapeDtypeStruct((TOK, D), BF16), in...  80.4 us
    unnamed x1, local copies, waits for them, and re-layouts  1.72 us

profile of v6, /device:TPU:1, one launch (start us, length us, event | category | flops | bytes accessed | tf_op | source)
XLA Modules:
  0.0 82.2 jit_solution(1749271520659769568)
XLA Ops:
  0.0 80.4 %shard_map.100 = bf16[128,1280]{1,0:T(8,128)(2,1)} custom-call(bf16[128,1280]{1,0:T(8,128)(2,1)} %bitcast.13, s32[1,128]{1,0:T(1,128)} %seg_h.1, s32[2,128]{1,0:T(2,128)} %bitcast.14, f32[2,128]{1,0:T(2,128)} %bitcast.15, f32[1280]{0:T(1024)} %lna_h.1, f32[1280]{0:T(1024)} %lne_h.1, bf16[1280,3840]{1,0:T(8,128)(2,1)} %wqkv_h.1, bf16[1280,1280]{1,0:T(8,128)(2,1)} %wao_h.1, ...), custom_call_target="tpu_custom_call" | custom-call | flops 14000000000 | bytes 24000000 | tf_op jit(solution)/shard_map/pallas_call | solution.py:665
  80.4 1.7 %copy.12 = bf16[1,128,1280]{2,1,0:T(8,128)(2,1)} copy(bf16[1,128,1280]{2,1,0:T(8,128)(2,1)} %bitcast.10) | data formatting | bytes 655360

commit v7 on v6

--- a/solution.py
+++ b/solution.py
@@ -78,7 +78,7 @@
     tok_h, seg_h, eid_h, gate_h, lna_h, lne_h, wqkv_h, wao_h, win_h, wout_h, out,
     tok, seg, eid, gate, lna, lne, wqkv, wao, win, wout, xn, xraw, info, q, k, v, ctx, ctxb, mid, xp, g, send, rcv, a, hid,
     part, keep, own, stage, back, rst, pack, ret, unp0, unp1, pkm0, pkm1, gcol,
-    zx, gf, fsend, frcv, unf, pkf, frst, fpack, fret, fpart, fout, fown, fstage, fback,
+    zx, gf, fsend, frcv, unf, pkf, frst, fpack, fret, facc, pacc, fpart, fout, fown, fstage, fback,
     i_sem, w_sem, as_sem, ar_sem, ss_sem, sr_sem, ds_sem, dr_sem, zs_sem, zr_sem, bs_sem, br_sem,
     es_sem, er_sem, round_sem, xs_sem, xr_sem, fds_sem, fdr_sem, fes_sem, fer_sem, ys_sem, yr_sem,
 ):
@@ -100,10 +100,10 @@
         return xs[sign * dx % 4] + ys[sign * dy % 4] + cs[dc]
 
     def rows_of(j):
-        return pl.ds(pl.multiple_of(j * MSG, MSG), MSG)
+        return pl.ds(j * MSG, MSG)
 
     def frows_of(j):
-        return pl.ds(pl.multiple_of(j * FMSG, FMSG), FMSG)
+        return pl.ds(j * FMSG, FMSG)
 
     small = [(tok_h, tok), (lna_h, lna), (eid_h, eid), (seg_h, seg), (gate_h, gate), (lne_h, lne)]
     small = [pltpu.make_async_copy(src, dst, i_sem.at[n]) for n, (src, dst) in enumerate(small)]
@@ -165,10 +165,14 @@
     named = jnp.where((ei == e0) | (ei == e1), 1.0, 0.0).astype(BF16)
     before = jnp.where(iota((TOK, TOK), 0) < iota((TOK, TOK), 1), 1.0, 0.0).astype(BF16)
     count = dot(named, before)
+    order = jnp.full((NE, TOK), NE - 1, I32)
+    for n in range(NE - 1):
+        order = jnp.where(ei == shifted(n, 1), n, order)
     chosen = []
     lines = [seg[...].astype(F32)]
     for e in (e0, e1):
         slot = jnp.sum(jnp.where(ei == e, count, 0.0), axis=0, keepdims=True).astype(I32)
+        e = jnp.sum(jnp.where(ei == e, order, 0), axis=0, keepdims=True)
         lines.append((e * FMSG + slot).astype(F32))
         odd = slot & 1
         pair = e * MSG + 3 * CAP + lax.shift_right_logical(slot, 1)
@@ -218,8 +222,6 @@
             at = jnp.where(cc < 3, at, jnp.where((slot & 1) == cc - 3, pair, -1))
         ref[...] = jnp.where(r == at, 1.0, 0.0).astype(BF16)
 
-    fixed(unp0, 0, 64, 0, 0, MSG)
-    fixed(unp1, 0, 80, 64, 7 * MSG, MSG)
 
     r0.wait_recv()
     ro.start()
@@ -249,10 +251,6 @@
         each(NC, step)
 
     keys_values(0, TOK)
-    fixed(pkm0, 1, 80, 0, 0, MSG)
-    fixed(pkm1, 1, 80, 64, GM, MSG)
-    fixed(unf, 0, CR, 0, 0, FMSG)
-    fixed(pkf, 1, CR, 0, 0, FMSG)
 
     r1.wait_recv()
     l0.wait_recv()
@@ -265,16 +263,6 @@
     key_kind = jnp.concatenate(kinds, axis=1)
     same = lax.dot_general(kinds[0], key_kind, (((0,), (0,)), ((), ())), preferred_element_type=F32)
     bias = jnp.where(same > 0.5, 0.0, NEG)
-
-    for s in range(4):
-        more = jnp.zeros((8, TOK), F32)
-        if s == 0:
-            more = stacked_lines([row.astype(F32) for kind in chosen for row in kind])
-        square = jnp.concatenate([info[s], more, jnp.zeros((TOK - 16, TOK), F32)], axis=0)
-        gcol[s] = jnp.transpose(square)
-        r = iota((ALLF, TOK), 0) - CAP * s
-        f0, f1 = info[s, 1:2, :].astype(I32), info[s, 2:3, :].astype(I32)
-        gf[:, s * TOK : (s + 1) * TOK] = jnp.where((r == f0) | (r == f1), 1.0, 0.0).astype(BF16)
 
     ro.wait_recv()
     lo.wait_recv()
@@ -339,7 +327,6 @@
         rows = pl.ds(i * 256, 256)
         send[rows, :] = dot(g[rows, :], xp[...]).astype(BF16)
 
-    each(ALL // 256, fill)
 
     pl.semaphore_wait(round_sem.at[1], 1)
 
@@ -347,17 +334,28 @@
         for n in range(first, last):
             dest = shifted(n, 1)
             remote(
-                send.at[rows_of(dest), :], rcv.at[rows_of(n), :],
+                send.at[rows_of(n), :], rcv.at[rows_of(n), :],
                 ds_sem, dr_sem.at[n // GS], (dest, z),
             ).start()
 
-    to_experts(0, HALF)
+    for i in range(2):
+        fill(i)
+        to_experts(i * GS, (i + 1) * GS)
     xr0.wait_recv()
     xro.start()
     xl1.wait_recv()
     xlo.start()
-    to_experts(HALF, NE - 1)
-    rcv[pl.ds((NE - 1) * MSG, MSG), :] = send[rows_of(d), :]
+    for i in range(2, 4):
+        fill(i)
+        to_experts(i * GS, min((i + 1) * GS, NE - 1))
+    rcv[rows_of(NE - 1), :] = send[rows_of(NE - 1), :]
+
+    fixed(unp0, 0, 64, 0, 0, MSG)
+    fixed(unp1, 0, 80, 64, 7 * MSG, MSG)
+    for s in range(4):
+        r = iota((ALLF, TOK), 0) - CAP * s
+        f0, f1 = info[s, 1:2, :].astype(I32), info[s, 2:3, :].astype(I32)
+        gf[:, s * TOK : (s + 1) * TOK] = jnp.where((r == f0) | (r == f1), 1.0, 0.0).astype(BF16)
 
     def piece_of(slot, half, n):
         first, number = OUT[n]
@@ -462,20 +460,28 @@
         zc["l", 0, n].start()
     for copy in (xr1, xl0, xro, xlo):
         copy.wait_recv()
-    for i in range(ALLF // 256):
-        rows = pl.ds(i * 256, 256)
+    for half in range(2):
+        rows = pl.ds(half * HALF * FMSG, HALF * FMSG)
         fsend[rows, :] = dot(gf[rows, :], zx[...]).astype(BF16)
-    for n in range(NE - 1):
-        dest = shifted(n, 1)
-        remote(
-            fsend.at[frows_of(dest), :], frcv.at[frows_of(n), :],
-            fds_sem, fdr_sem.at[n // HALF], (dest, z),
-        ).start()
-    frcv[pl.ds((NE - 1) * FMSG, FMSG), :] = fsend[frows_of(d), :]
+        for n in range(half * HALF, min((half + 1) * HALF, NE - 1)):
+            dest = shifted(n, 1)
+            remote(
+                fsend.at[frows_of(n), :], frcv.at[frows_of(n), :],
+                fds_sem, fdr_sem.at[half], (dest, z),
+            ).start()
+    frcv[frows_of(NE - 1), :] = fsend[frows_of(NE - 1), :]
     for n in range(2):
         unpack(1, n)
         zc["r", 1, n].start()
         zc["l", 1, n].start()
+
+    for s in range(4):
+        more = jnp.zeros((8, TOK), F32)
+        if s == 0:
+            more = stacked_lines([row.astype(F32) for kind in chosen for row in kind])
+        square = jnp.concatenate([info[s], more, jnp.zeros((TOK - 16, TOK), F32)], axis=0)
+        gcol[s] = jnp.transpose(square)
+    fixed(unf, 0, CR, 0, 0, FMSG)
 
     ri = iota((TOK, ALL), 1)
     for cc in range(NC):
@@ -492,9 +498,12 @@
         for kind in range(2):
             at = gcol[s, :, 1 + kind : 2 + kind].astype(I32) + CAP * s
             fpick[pl.ds(s * 256 + kind * TOK, TOK), :] = jnp.where(fi == at, 1.0, 0.0).astype(BF16)
+    fixed(pkf, 1, CR, 0, 0, FMSG)
     for n in range(2):
         zc["l", 1, n].wait_recv()
         zc["lo", n].start()
+    fixed(pkm0, 1, 80, 0, 0, MSG)
+    fixed(pkm1, 1, 80, 64, GM, MSG)
 
     def funpack(half):
         number = HALF if half == 0 else HALF - 1
@@ -509,7 +518,8 @@
         for m in range(half * HALF, min((half + 1) * HALF, NE - 1)):
             dest = shifted(m, -1)
             remote(
-                fpack.at[frows_of(m), :], fret.at[frows_of(d), :], fes_sem, fer_sem, (dest, z)
+                fpack.at[frows_of(m), :], fret.at[frows_of(m), :],
+                fes_sem, fer_sem.at[half], (dest, z),
             ).start()
 
     funpack(0)
@@ -537,7 +547,7 @@
     expert(1, 1, into_keep(1))
     expert(0, 1, into_own(1))
     freturn(1)
-    fret[frows_of(d), :] = fpack[pl.ds((NE - 1) * FMSG, FMSG), :]
+    fret[frows_of(NE - 1), :] = fpack[frows_of(NE - 1), :]
     for n in range(2):
         first, number = BACK[n]
         rows = pl.ds(first, number)
@@ -592,32 +602,42 @@
             for m in range(group * GS, min((group + 1) * GS, NE - 1)):
                 dest = shifted(m, -1)
                 remote(
-                    pack.at[rows_of(m), :], ret.at[rows_of(d), :], es_sem, er_sem, (dest, z)
+                    pack.at[rows_of(m), :], ret.at[rows_of(m), :],
+                    es_sem, er_sem.at[group], (dest, z),
                 ).start()
+    def fhalf(half):
+        number = HALF if half == 0 else HALF - 1
+        got = fret.at[pl.ds(half * HALF * FMSG, number * FMSG), :]
+        remote(got, got, fes_sem, fer_sem.at[half], right).wait_recv()
+
+    early = pl.ds(0, HALF * FMSG)
+    late = pl.ds(HALF * FMSG, HALF * FMSG)
+    fhalf(0)
+    facc[...] = dot(fpick[:, early], fret[early, :])
     finish(0)
-
-    others = fret.at[pl.ds(0, (NE - 1) * FMSG), :]
-    remote(others, others, fes_sem, fer_sem, right).wait_recv()
-    for s in (3, 1, 2, 0):
-        both = dot(fpick[pl.ds(s * 256, 256), :], fret[...])
-        sums = gcol[s, :, 3:4] * both[:TOK] + gcol[s, :, 4:5] * both[TOK:]
+    fhalf(1)
+
+    def weighted(both, s):
+        return gcol[s, :, 3:4] * both[:TOK] + gcol[s, :, 4:5] * both[TOK:]
+
+    rows = pl.ds(3 * 256, 256)
+    fout[3] = weighted(facc[rows, :] + dot(fpick[rows, late], fret[late, :]), 3).astype(BF16)
+    ya0.start()
+    ya1.start()
+    rows = pl.ds(0, 3 * 256)
+    both = facc[rows, :] + dot(fpick[rows, late], fret[late, :])
+    for s in range(3):
+        sums = weighted(both[s * 256 : (s + 1) * 256], s)
         if s == 0:
             fown[...] = sums
         else:
             fpart[s] = sums
-            for n in range(2):
-                rows = pl.ds(n * 64, 64)
-                fout[s, rows] = sums[n * 64 : (n + 1) * 64].astype(BF16)
-        if s == 3:
-            ya0.start()
-            ya1.start()
-        if s == 1:
-            yl0.start()
-        if s == 2:
-            yr1.start()
+            fout[s] = sums.astype(BF16)
+    yl0.start()
+    yr1.start()
 
     finish(1)
-    ret[rows_of(d), :] = pack[pl.ds((NE - 1) * MSG, MSG), :]
+    ret[rows_of(NE - 1), :] = pack[rows_of(NE - 1), :]
 
     ya0.wait_recv()
     fout[2, pl.ds(0, 64)] = (fpart[2, pl.ds(0, 64)] + fstage[0].astype(F32)).astype(BF16)
@@ -626,14 +646,22 @@
     fout[1, pl.ds(64, 64)] = (fpart[1, pl.ds(64, 64)] + fstage[1].astype(F32)).astype(BF16)
     yl1.start()
 
-    others = ret.at[pl.ds(0, (NE - 1) * MSG), :]
-    remote(others, others, es_sem, er_sem, right).wait_recv()
+    def returned(group):
+        number = GS if group < 3 else GS - 1
+        got = ret.at[pl.ds(group * GM, number * MSG), :]
+        remote(got, got, es_sem, er_sem.at[group], right).wait_recv()
+        return pl.ds(group * GM, GM)
+
+    first, second = returned(0), returned(2)
+    pacc[...] = dot(pick[:, first], ret[first, :]) + dot(pick[:, second], ret[second, :])
+    first, second = returned(1), returned(3)
+    picked = dot(pick[:, first], ret[first, :]) + dot(pick[:, second], ret[second, :])
+    picked = pacc[...] + picked
     g0, g1 = gcol[0, :, 3:4], gcol[0, :, 4:5]
     for cc in range(3):
-        both = dot(pick[pl.ds(cc * 256, 256), :], ret[...])
+        both = picked[cc * 256 : (cc + 1) * 256]
         out[:, cols(cc)] = (mid[:, cols(cc)] + g0 * both[:TOK] + g1 * both[TOK:]).astype(BF16)
-    even = dot(pick[pl.ds(3 * 256, 256), :], ret[...])[:, :128]
-    both = even + dot(pick[pl.ds(4 * 256, 256), :], ret[...])[:, 128:]
+    both = picked[3 * 256 : 4 * 256, :128] + picked[4 * 256 :, 128:]
     out[:, 3 * COL : PW] = (
         mid[:, 3 * COL : PW] + g0 * both[:TOK] + g1 * both[TOK:]
     ).astype(BF16)
@@ -650,11 +678,11 @@
     gone = send.at[pl.ds(0, (NE - 1) * MSG), :]
     remote(gone, gone, ds_sem, dr_sem.at[0], right).wait_send()
     gone = pack.at[pl.ds(0, (NE - 1) * MSG), :]
-    remote(gone, gone, es_sem, er_sem, right).wait_send()
+    remote(gone, gone, es_sem, er_sem.at[0], right).wait_send()
     gone = fsend.at[pl.ds(0, (NE - 1) * FMSG), :]
     remote(gone, gone, fds_sem, fdr_sem.at[0], right).wait_send()
     gone = fpack.at[pl.ds(0, (NE - 1) * FMSG), :]
-    remote(gone, gone, fes_sem, fer_sem, right).wait_send()
+    remote(gone, gone, fes_sem, fer_sem.at[0], right).wait_send()
 
 
 def layer(tok, seg, eid, gate, lna, lne, wqkv, wao, win, wout):
@@ -715,6 +743,8 @@
             V((2, 4 * CR, FW), BF16),
             V((ALLF, FW), BF16),
             V((ALLF, FW), BF16),
+            V((4 * 256, FW), F32),
+            V((NC * 256, COL), F32),
             V((4, TOK, FW), F32),
             V((4, TOK, FW), BF16),
             V((TOK, FW), F32),
@@ -733,14 +763,14 @@
             dma((10,)),
             dma((10,)),
             dma,
-            dma,
+            dma((4,)),
             pltpu.SemaphoreType.REGULAR((2,)),
             dma((6,)),
             dma((6,)),
             dma,
             dma((2,)),
             dma,
-            dma,
+            dma((2,)),
             dma((6,)),
             dma((6,)),
         ],

time: 82.3 us -> 80.6 us (0.979)
  Pallas kernels: 80.4 us -> 78.7 us
    pallas_call x1, Pallas kernels: 80.4 us -> 78.7 us  [layer(): pl.pallas_call(kernel, out_shape=jax.ShapeDtypeStruct((TOK, D), BF16), in...]
where the time goes in v7:
time: 80.6 us; the launch traced here: 80.5 us
  Pallas kernels  78.7 us (98%)
  local copies, waits for them, and re-layouts  1.72 us (2%)
    pallas_call x1, Pallas kernels, layer(): pl.pallas_call(kernel, out_shape=jax.ShapeDtypeStruct((TOK, D), BF16), in...  78.7 us
    unnamed x1, local copies, waits for them, and re-layouts  1.72 us

profile of v7, /device:TPU:1, one launch (start us, length us, event | category | flops | bytes accessed | tf_op | source)
XLA Modules:
  0.0 80.5 jit_solution(17281485377519397107)
XLA Ops:
  0.0 78.7 %shard_map.100 = bf16[128,1280]{1,0:T(8,128)(2,1)} custom-call(bf16[128,1280]{1,0:T(8,128)(2,1)} %bitcast.13, s32[1,128]{1,0:T(1,128)} %seg_h.1, s32[2,128]{1,0:T(2,128)} %bitcast.14, f32[2,128]{1,0:T(2,128)} %bitcast.15, f32[1280]{0:T(1024)} %lna_h.1, f32[1280]{0:T(1024)} %lne_h.1, bf16[1280,3840]{1,0:T(8,128)(2,1)} %wqkv_h.1, bf16[1280,1280]{1,0:T(8,128)(2,1)} %wao_h.1, ...), custom_call_target="tpu_custom_call" | custom-call | flops 14000000000 | bytes 24000000 | tf_op jit(solution)/shard_map/pallas_call | solution.py:693
  78.7 1.7 %copy.12 = bf16[1,128,1280]{2,1,0:T(8,128)(2,1)} copy(bf16[1,128,1280]{2,1,0:T(8,128)(2,1)} %bitcast.10) | data formatting | bytes 655360

commit v8 on v7

--- a/solution.py
+++ b/solution.py
@@ -75,11 +75,11 @@
 
 
 def kernel(
-    tok_h, seg_h, eid_h, gate_h, lna_h, lne_h, wqkv_h, wao_h, win_h, wout_h, out,
-    tok, seg, eid, gate, lna, lne, wqkv, wao, win, wout, xn, xraw, info, q, k, v, ctx, ctxb, mid, xp, g, send, rcv, a, hid,
+    tok_h, seg_h, eid_h, gate_h, lna_h, lne_h, wqkv_h, wao_h, win_h, wout_h, out_h,
+    out,    tok, seg, eid, gate, lna, lne, wqkv, wao, win, wout, xn, xraw, info, q, k, v, ctx, ctxb, mid, xp, g, send, rcv, a, hid,
     part, keep, own, stage, back, rst, pack, ret, unp0, unp1, pkm0, pkm1, gcol,
     zx, gf, fsend, frcv, unf, pkf, frst, fpack, fret, facc, pacc, fpart, fout, fown, fstage, fback,
-    i_sem, w_sem, as_sem, ar_sem, ss_sem, sr_sem, ds_sem, dr_sem, zs_sem, zr_sem, bs_sem, br_sem,
+    i_sem, o_sem, w_sem, as_sem, ar_sem, ss_sem, sr_sem, ds_sem, dr_sem, zs_sem, zr_sem, bs_sem, br_sem,
     es_sem, er_sem, round_sem, xs_sem, xr_sem, fds_sem, fdr_sem, fes_sem, fer_sem, ys_sem, yr_sem,
 ):
     pick = wqkv.at[:, pl.ds(0, ALL)]
@@ -514,13 +514,15 @@
             a[s, half, :, PW:] = rows[s * CR : (s + 1) * CR]
 
     def freturn(half):
-        fpack[pl.ds(half * HALF * FMSG, HALF * FMSG), :] = dot(pkf[...], frst[half]).astype(BF16)
-        for m in range(half * HALF, min((half + 1) * HALF, NE - 1)):
-            dest = shifted(m, -1)
-            remote(
-                fpack.at[frows_of(m), :], fret.at[frows_of(m), :],
-                fes_sem, fer_sem.at[half], (dest, z),
-            ).start()
+        for group in (2 * half, 2 * half + 1):
+            rows = pl.ds((group - 2 * half) * FGM, FGM)
+            fpack[pl.ds(group * FGM, FGM), :] = dot(pkf[rows, :], frst[half]).astype(BF16)
+            for m in range(group * GS, min((group + 1) * GS, NE - 1)):
+                dest = shifted(m, -1)
+                remote(
+                    fpack.at[frows_of(m), :], fret.at[frows_of(m), :],
+                    fes_sem, fer_sem.at[half], (dest, z),
+                ).start()
 
     funpack(0)
     expert(1, 0, into_part(0))
@@ -665,11 +667,18 @@
     out[:, 3 * COL : PW] = (
         mid[:, 3 * COL : PW] + g0 * both[:TOK] + g1 * both[TOK:]
     ).astype(BF16)
+    leave = [
+        pltpu.make_async_copy(out.at[:, at], out_h.at[:, at], o_sem.at[n])
+        for n, at in enumerate((pl.ds(0, PW), pl.ds(PW, FW)))
+    ]
+    leave[0].start()
     for copy in (yl0, yr1, yr0, yl1):
         copy.wait_recv()
     out[:, PW:] = (
         mid[:, PW:] + fown[...] + fback[0].astype(F32) + fback[1].astype(F32)
     ).astype(BF16)
+
+    leave[1].start()
 
     for copy in seg_copies + [r0, r1, l0, l1, ro, lo] + ring + list(zc.values()):
         copy.wait_send()
@@ -683,10 +692,11 @@
     remote(gone, gone, fds_sem, fdr_sem.at[0], right).wait_send()
     gone = fpack.at[pl.ds(0, (NE - 1) * FMSG), :]
     remote(gone, gone, fes_sem, fer_sem.at[0], right).wait_send()
+    for copy in leave:
+        copy.wait()
 
 
 def layer(tok, seg, eid, gate, lna, lne, wqkv, wao, win, wout):
-    vm = pl.BlockSpec(memory_space=pltpu.VMEM)
     hbm = pl.BlockSpec(memory_space=pl.ANY)
     V = pltpu.VMEM
     dma = pltpu.SemaphoreType.DMA
@@ -694,8 +704,9 @@
         kernel,
         out_shape=jax.ShapeDtypeStruct((TOK, D), BF16),
         in_specs=[hbm] * 10,
-        out_specs=vm,
+        out_specs=hbm,
         scratch_shapes=[
+            V((TOK, D), BF16),
             V((TOK, D), BF16),
             V((1, TOK), I32),
             V((2, TOK), I32),
@@ -751,6 +762,7 @@
             V((2, 64, FW), BF16),
             V((2, TOK, FW), BF16),
             dma((6,)),
+            dma((2,)),
             dma((6,)),
             dma((6,)),
             dma((6,)),

time: 80.6 us -> 80.4 us (level)
  no operation moved by 1% of the time
where the time goes in v8:
time: 80.4 us; the launch traced here: 80.3 us
  Pallas kernels  78.6 us (98%)
  local copies, waits for them, and re-layouts  1.72 us (2%)
    pallas_call x1, Pallas kernels, layer(): pl.pallas_call(kernel, out_shape=jax.ShapeDtypeStruct((TOK, D), BF16), in...  78.6 us
    unnamed x1, local copies, waits for them, and re-layouts  1.72 us

profile of v8, /device:TPU:1, one launch (start us, length us, event | category | flops | bytes accessed | tf_op | source)
XLA Modules:
  0.0 80.3 jit_solution(131565969198804707)
XLA Ops:
  0.0 78.6 %shard_map.100 = bf16[128,1280]{1,0:T(8,128)(2,1)} custom-call(bf16[128,1280]{1,0:T(8,128)(2,1)} %bitcast.13, s32[1,128]{1,0:T(1,128)} %seg_h.1, s32[2,128]{1,0:T(2,128)} %bitcast.14, f32[2,128]{1,0:T(2,128)} %bitcast.15, f32[1280]{0:T(1024)} %lna_h.1, f32[1280]{0:T(1024)} %lne_h.1, bf16[1280,3840]{1,0:T(8,128)(2,1)} %wqkv_h.1, bf16[1280,1280]{1,0:T(8,128)(2,1)} %wao_h.1, ...), custom_call_target="tpu_custom_call" | custom-call | flops 14000000000 | bytes 24000000 | tf_op jit(solution)/shard_map/pallas_call | solution.py:703
  78.6 1.7 %copy.12 = bf16[1,128,1280]{2,1,0:T(8,128)(2,1)} copy(bf16[1,128,1280]{2,1,0:T(8,128)(2,1)} %bitcast.10) | data formatting | bytes 655360
